TPU v7x, 32 devices: a whole 2x2x4 slice. The times are simulated.
32 devices in a mesh: fsdp: 4 (over y, core), blk: 2 (over x), seq: 4 (over z).
Axes of the slice: x: 2, y: 2, z: 4, core: 2. Of those that a mesh axis runs over, the one named last changes fastest.
Arguments:
- tokens: float32 [4, 1024, 768], P('fsdp', ('blk', 'seq')), may hold values from -6 to 6
- counts: int32 [4, 8], P('fsdp'), may hold values from 1 to 128, 820 in all within a row
- norm_gain: bfloat16 [2, 768], replicated, may hold values from 0.5 to 1.5
- norm_bias: bfloat16 [2, 768], replicated, may hold values from -4 to 4
- vec_bias: bfloat16 [4, 768], replicated, may hold values from -4 to 4
- up_bias: bfloat16 [3072], replicated, may hold values from -6 to 6
- w_qkv: bfloat16 [768, 2304], P('fsdp'), may hold values from -0.3125 to 0.3125
- w_out: bfloat16 [768, 768], P('fsdp'), may hold values from -1.25 to 1.25
- w_up: bfloat16 [768, 3072], P('fsdp'), may hold values from -0.21875 to 0.21875
- w_down: bfloat16 [3072, 768], P('fsdp'), may hold values from -0.109375 to 0.109375
- grad_out: float32 [4, 1024, 768], P('fsdp', ('blk', 'seq')), may hold values from -6 to 6
Outputs:
- activations: float32 [4, 1024, 768], P('fsdp', ('blk', 'seq'))
- grad_tokens: float32 [4, 1024, 768], P('fsdp', ('blk', 'seq'))
- grad_norm_gain: float32 [2, 768], P(None, 'fsdp')
- grad_norm_bias: float32 [2, 768], P(None, 'fsdp')
- grad_vec_bias: float32 [4, 768], P(None, 'fsdp')
- grad_up_bias: float32 [3072], P('fsdp')
- grad_w_qkv: float32 [768, 2304], P('fsdp')
- grad_w_out: float32 [768, 768], P('fsdp')
- grad_w_up: float32 [768, 3072], P('fsdp')
- grad_w_down: float32 [3072, 768], P('fsdp')
Inputs may be any that keep to these rules, and one draw needn't show every extreme that they name: `counts`: row i lists, for the 8 devices that hold image i in order, how many of their 128 slots carry tokens; these come first. A row sums to 820 and holds 128 at least once.
All inputs are finite; a program needn't handle non-finite values.
Results may differ from a plain program's by a relative error of at most 0.02.
Values may be sent and summed in bfloat16 or wider, within the bound.
No kernel may reach another device: no remote copies, remote signals or barrier semaphores. Data moves between devices by JAX's collectives and lax.ppermute only.
A program may use at most 128 MiB of HBM per device.

v0:
```python
import functools

import jax
import jax.numpy as jnp
from jax import lax
from jax.experimental import pallas as pl
from jax.experimental.pallas import tpu as pltpu
from jax.sharding import PartitionSpec as P

HD = 64
EPSILON = 1e-06
MASKED = -1e30
SCALE = HD ** (-0.5)
BF = jnp.bfloat16
F32 = jnp.float32
VMEM_LIMIT = 44 * 1024 * 1024


def dot_nn(left_side, right_side):
    return lax.dot_general(
        left_side, right_side, (((1,), (0,)), ((), ())), preferred_element_type=F32
    )


def dot_nt(left_side, right_side):
    return lax.dot_general(
        left_side, right_side, (((1,), (1,)), ((), ())), preferred_element_type=F32
    )


def dot_tn(left_side, right_side):
    return lax.dot_general(
        left_side, right_side, (((0,), (0,)), ((), ())), preferred_element_type=F32
    )


def swap(array, axis, bits):
    return lax.ppermute(array, axis, [(i, i ^ bits) for i in range(lax.axis_size(axis))])


def from_all(array, axis):
    return [array] + [swap(array, axis, j) for j in range(1, lax.axis_size(axis))]


def doubled(array, axis):
    pieces = {0: array}
    bit = lax.axis_size(axis) // 2
    while bit:
        pieces.update({j | bit: swap(piece, axis, bit) for j, piece in list(pieces.items())})
        bit //= 2
    return [pieces[j] for j in range(lax.axis_size(axis))]


def piece_bias(counts_ref, first_piece, pieces, slot_rows):
    row = lax.broadcasted_iota(jnp.int32, (pieces * slot_rows, 1), 0)
    limit = jnp.zeros_like(row)
    for piece in range(pieces):
        end = counts_ref[first_piece + piece] + piece * slot_rows
        limit = jnp.where(row >= piece * slot_rows, end, limit)
    return jnp.where(row < limit, 0.0, MASKED)


def attend_kernel(blocks, heads, pieces, slot_rows, counts_ref, q_ref, *refs):
    kv_refs, (out_ref, log_ref) = refs[:blocks], refs[blocks:]
    width = heads * HD
    biases = [piece_bias(counts_ref, m * pieces, pieces, slot_rows) for m in range(blocks)]
    for head in range(heads):
        low, high = head * HD, (head + 1) * HD
        query = q_ref[:, low:high] * SCALE
        scores = [dot_nt(kv[:, low:high], query) + bias for kv, bias in zip(kv_refs, biases)]
        top = functools.reduce(
            jnp.maximum, [jnp.max(block, axis=0, keepdims=True) for block in scores]
        )
        powers = [jnp.exp(block - top) for block in scores]
        total = sum(jnp.sum(block, axis=0, keepdims=True) for block in powers)
        inverse = 1.0 / total
        result = sum(
            dot_tn((block * inverse).astype(BF), kv[:, width + low : width + high])
            for block, kv in zip(powers, kv_refs)
        )
        out_ref[:, low:high] = result.astype(BF)
        log_ref[head : head + 1, :] = top + jnp.log(total)


def attend_back_kernel(blocks, heads, pieces, slot_rows, counts_ref, q_ref, log_ref, d_ref, *refs):
    kv_refs, dq_ref, dkv_refs = refs[:blocks], refs[blocks], refs[blocks + 1 :]
    width = heads * HD
    biases = [piece_bias(counts_ref, m * pieces, pieces, slot_rows) for m in range(blocks)]
    for head in range(heads):
        low, high = head * HD, (head + 1) * HD
        query = q_ref[:, low:high] * SCALE
        d_out = d_ref[:, low:high]
        log_row = log_ref[head : head + 1, :]
        softs, d_softs, delta = [], [], 0.0
        for kv, bias in zip(kv_refs, biases):
            soft = jnp.exp(dot_nt(kv[:, low:high], query) + bias - log_row)
            d_soft = dot_nt(kv[:, width + low : width + high], d_out)
            delta = delta + jnp.sum(soft * d_soft, axis=0, keepdims=True)
            softs.append(soft)
            d_softs.append(d_soft)
        d_query = 0.0
        for kv, dkv, soft, d_soft in zip(kv_refs, dkv_refs, softs, d_softs):
            d_scores = (soft * (d_soft - delta)).astype(BF)
            d_query = d_query + dot_tn(d_scores, kv[:, low:high])
            dkv[:, low:high] = dot_nn(d_scores, query).astype(dkv.dtype)
            dkv[:, width + low : width + high] = dot_nn(soft.astype(BF), d_out).astype(dkv.dtype)
        dq_ref[:, low:high] = (d_query * SCALE).astype(BF)


def attend(counts, queries, kv_blocks, slot_rows):
    rows, width = queries.shape
    blocks, heads = len(kv_blocks), width // HD
    pieces = kv_blocks[0].shape[0] // slot_rows
    return pl.pallas_call(
        functools.partial(attend_kernel, blocks, heads, pieces, slot_rows),
        out_shape=(
            jax.ShapeDtypeStruct((rows, width), BF),
            jax.ShapeDtypeStruct((heads, rows), F32),
        ),
        in_specs=[pl.BlockSpec(memory_space=pltpu.SMEM)]
        + [pl.BlockSpec(memory_space=pltpu.VMEM)] * (1 + blocks),
        out_specs=(pl.BlockSpec(memory_space=pltpu.VMEM),) * 2,
        compiler_params=pltpu.CompilerParams(vmem_limit_bytes=VMEM_LIMIT),
        cost_estimate=pl.CostEstimate(
            flops=4 * rows * blocks * rows * width,
            bytes_accessed=2 * rows * width * (2 + 2 * blocks),
            transcendentals=rows * rows * blocks * heads,
        ),
        name="attend",
    )(counts, queries, *kv_blocks)


def attend_back(counts, queries, log_total, d_out, kv_blocks, slot_rows):
    rows, width = queries.shape
    blocks, heads = len(kv_blocks), width // HD
    pieces = kv_blocks[0].shape[0] // slot_rows
    return pl.pallas_call(
        functools.partial(attend_back_kernel, blocks, heads, pieces, slot_rows),
        out_shape=(jax.ShapeDtypeStruct((rows, width), BF),)
        + tuple(
            jax.ShapeDtypeStruct(block.shape, F32 if m == 0 else BF)
            for m, block in enumerate(kv_blocks)
        ),
        in_specs=[pl.BlockSpec(memory_space=pltpu.SMEM)]
        + [pl.BlockSpec(memory_space=pltpu.VMEM)] * (3 + blocks),
        out_specs=(pl.BlockSpec(memory_space=pltpu.VMEM),) * (1 + blocks),
        compiler_params=pltpu.CompilerParams(vmem_limit_bytes=VMEM_LIMIT),
        cost_estimate=pl.CostEstimate(
            flops=10 * rows * blocks * rows * width,
            bytes_accessed=2 * rows * width * (3 + 5 * blocks),
            transcendentals=rows * rows * blocks * heads,
        ),
        name="attend_back",
    )(counts, queries, log_total, d_out, *kv_blocks)


def normalised(matrix_rows):
    centre = matrix_rows - jnp.mean(matrix_rows, axis=-1, keepdims=True)
    inverse = lax.rsqrt(jnp.mean(centre * centre, axis=-1, keepdims=True) + EPSILON)
    return centre * inverse, inverse


def norm_back(upstream, unit_rows, inverse, gain_row):
    scaled = upstream * gain_row
    d_rows = inverse * (
        scaled
        - jnp.mean(scaled, axis=-1, keepdims=True)
        - unit_rows * jnp.mean(scaled * unit_rows, axis=-1, keepdims=True)
    )
    return d_rows, jnp.sum(upstream * unit_rows, axis=0), jnp.sum(upstream, axis=0)


def after(value, *others):
    return lax.optimization_barrier((value, others))[0]


def take(array, index, size=1):
    return lax.dynamic_slice_in_dim(array, index, size, axis=0)


def core_sums(grads, own):
    owners, rows, columns = grads.shape
    pairs = grads.reshape(owners // 2, 2, rows, columns)
    bit = own % 2
    sent = lax.dynamic_slice_in_dim(pairs, 1 - bit, 1, axis=1)[:, 0]
    kept = lax.dynamic_slice_in_dim(pairs, bit, 1, axis=1)[:, 0]
    return kept.astype(F32) + swap(sent.astype(BF), "fsdp", 1).astype(F32)


def owner_sums(halved, own):
    bit = 2
    while bit < lax.axis_size("fsdp"):
        pairs = halved.reshape(halved.shape[0] // 2, 2, *halved.shape[1:])
        high = (own // bit) % 2
        sent = lax.dynamic_slice_in_dim(pairs, 1 - high, 1, axis=1)[:, 0]
        kept = lax.dynamic_slice_in_dim(pairs, high, 1, axis=1)[:, 0]
        halved = kept + swap(sent.astype(BF), "fsdp", bit).astype(F32)
        bit *= 2
    return halved[0]


def chunk_sums(array, axis, index):
    count = lax.axis_size(axis)
    rows = array.shape[0] // count
    total = take(array, index * rows, rows)
    for j in range(1, count):
        sent = take(array, (index ^ j) * rows, rows).astype(BF)
        total = total + swap(sent, axis, j).astype(F32)
    return total.astype(BF)


def split_sums(array, axis):
    count = lax.axis_size(axis)
    rows = array.shape[0] // count
    own = array[:rows].astype(F32)
    for j in range(1, count):
        own = own + swap(array[j * rows : (j + 1) * rows].astype(BF), axis, j).astype(F32)
    return own


def sum_over(array, axes):
    for name in axes:
        bit = 1
        while bit < lax.axis_size(name):
            array = array + swap(array, name, bit)
            bit *= 2
    return array


def in_order(pieces, index):
    result = []
    for place in range(len(pieces)):
        chosen = pieces[place]
        for other in range(1, len(pieces)):
            chosen = jnp.where(index == other, pieces[place ^ other], chosen)
        result.append(chosen)
    return result


def place_kernel(seqs, blocks, layouts, place_ref, *refs):
    pieces = refs[: blocks * seqs]
    outs = refs[blocks * seqs : -2]
    held, sems = refs[-2:]
    blk, seq = place_ref[0], place_ref[1]
    copies = [
        pltpu.make_async_copy(
            pieces[m * seqs + k],
            held.at[jnp.bitwise_xor(blk, m), jnp.bitwise_xor(seq, k)],
            sems.at[m * seqs + k],
        )
        for m in range(blocks)
        for k in range(seqs)
    ]
    for copy in copies:
        copy.start()
    for copy in copies:
        copy.wait()
    for out, spots in zip(outs, layouts):
        for b in range(blocks):
            for k in range(seqs):
                for first, size, row, column in spots(b, k):
                    piece = held[b, k, :, first : first + size]
                    out[row : row + piece.shape[0], column : column + size] = piece.astype(F32)


def put_in_place(pieces, blk, seq, shapes, layouts, label):
    blocks, seqs = len(pieces), len(pieces[0])
    piece = pieces[0][0]
    return pl.pallas_call(
        functools.partial(place_kernel, seqs, blocks, layouts),
        out_shape=tuple(jax.ShapeDtypeStruct(shape, F32) for shape in shapes),
        in_specs=[pl.BlockSpec(memory_space=pltpu.SMEM)]
        + [pl.BlockSpec(memory_space=pl.ANY)] * (blocks * seqs),
        out_specs=(pl.BlockSpec(memory_space=pltpu.VMEM),) * len(shapes),
        scratch_shapes=[
            pltpu.VMEM((blocks, seqs) + piece.shape, BF),
            pltpu.SemaphoreType.DMA((blocks * seqs,)),
        ],
        compiler_params=pltpu.CompilerParams(vmem_limit_bytes=VMEM_LIMIT),
        cost_estimate=pl.CostEstimate(
            flops=0, bytes_accessed=6 * blocks * seqs * piece.size, transcendentals=0
        ),
        name=label,
    )(jnp.stack([blk, seq]), *[one for row in pieces for one in row])


def shards(
    tokens, counts, norm_gain, norm_bias, vec_bias, up_bias, w_qkv, w_out, w_up, w_down, grad_out
):
    owners, blocks, seqs = (lax.axis_size(name) for name in ("fsdp", "blk", "seq"))
    own, blk, seq = (lax.axis_index(name) for name in ("fsdp", "blk", "seq"))
    rows, width = tokens.shape[1:]
    head_width = width // seqs
    own_rows = width // owners
    hidden_rows = w_down.shape[0] // blocks
    hidden_width = hidden_rows * owners
    out_width = width // blocks

    gains = norm_gain.astype(F32)
    shifts = norm_bias.astype(F32)
    biases = vec_bias.astype(F32)

    inputs = tokens[0]
    unit1, inverse1 = normalised(inputs)
    normed1 = (unit1 * gains[0] + shifts[0]).astype(BF)
    qkv_mine = jnp.concatenate(
        [
            lax.dynamic_slice_in_dim(w_qkv, part * width + seq * head_width, head_width, axis=1)
            for part in range(3)
        ],
        axis=1,
    )
    normed1_all = jnp.concatenate(from_all(normed1, "seq"))
    qkv_full = jnp.concatenate(in_order(doubled(qkv_mine, "fsdp"), own))

    full_out = lax.all_gather(w_out, "fsdp", axis=0, tiled=True)
    up_late, down_late, grad_late = after((w_up, w_down, grad_out), normed1, qkv_mine)
    up_mine = jnp.concatenate(
        [
            lax.dynamic_slice_in_dim(
                up_late, (i * blocks + blk) * hidden_rows, hidden_rows, axis=1
            )
            for i in range(owners)
        ],
        axis=1,
    )
    full_up = lax.all_gather(up_mine, "fsdp", axis=0, tiled=True)
    down_mine = take(down_late, blk * hidden_rows, hidden_rows)
    full_down = jnp.concatenate(in_order(doubled(down_mine, "fsdp"), own))
    up_shift = jnp.concatenate(
        [
            lax.dynamic_slice_in_dim(up_bias, (i * blocks + blk) * hidden_rows, hidden_rows)
            for i in range(owners)
        ]
    ).astype(F32)
    qkv_shift = jnp.concatenate(
        [
            lax.dynamic_slice_in_dim(biases[0], seq * head_width, head_width),
            jnp.zeros((head_width,), F32),
            lax.dynamic_slice_in_dim(biases[1], seq * head_width, head_width),
        ]
    )
    own_count = counts[0, blk * seqs + seq]
    own_valid = lax.broadcasted_iota(jnp.int32, (rows, 1), 0) < own_count
    key_counts = jnp.stack(
        [counts[0, (blk ^ m) * seqs + (seq ^ k)] for m in range(blocks) for k in range(seqs)]
    )
    grad_rows = jnp.where(own_valid, grad_late[0], 0.0)
    d_outcome = grad_rows.astype(BF)
    d_outcome_all = jnp.concatenate(from_all(d_outcome, "blk"))

    key_value = (
        dot_nn(normed1_all, qkv_full[:, head_width:]) + qkv_shift[head_width:]
    ).astype(BF)
    kv_blocks = from_all(key_value, "blk")
    queries = (
        dot_nn(after(normed1_all, key_value), qkv_full[:, :head_width]) + qkv_shift[:head_width]
    ).astype(BF)
    attended, log_total = attend(key_counts, queries, kv_blocks, rows)
    att_pieces = [attended[:rows]] + [
        swap(attended[k * rows : (k + 1) * rows], "seq", k) for k in range(1, seqs)
    ]
    token_att = jnp.concatenate(in_order(att_pieces, seq), axis=1)
    middle = inputs + dot_nn(token_att, full_out) + biases[2]
    unit2, inverse2 = normalised(middle)
    normed2 = (unit2 * gains[1] + shifts[1]).astype(BF)

    d_hidden = lax.optimization_barrier(dot_nt(after(d_outcome_all, normed2), full_down))
    normed2_all = jnp.concatenate(from_all(normed2, "blk"))
    up_proj = dot_nn(after(normed2_all, d_hidden), full_up) + up_shift
    chance = 0.5 * (1.0 + lax.erf(up_proj * (0.5**0.5)))
    hidden = (up_proj * chance).astype(BF)
    slope = chance + up_proj * (jnp.exp(-0.5 * up_proj * up_proj) * 0.3989422804014327)
    d_up = (d_hidden * slope).astype(BF)
    d_normed2_parts = dot_nt(d_up, full_up).astype(BF)
    d_normed2 = split_sums(d_normed2_parts, "blk")
    half_down = core_sums(
        dot_tn(after(hidden, d_normed2_parts), d_outcome_all).astype(BF).reshape(
            owners, hidden_rows, width
        ),
        own,
    )
    d_middle_norm, d_gain_two, d_shift_two = norm_back(d_normed2, unit2, inverse2, gains[1])
    d_middle = grad_rows + d_middle_norm
    d_branch = d_middle.astype(BF)
    d_head_pieces = [
        dot_nt(d_branch, take(full_out, (seq ^ k) * head_width, head_width)).astype(BF)
        for k in range(seqs)
    ]
    d_attended = jnp.concatenate(
        [d_head_pieces[0]] + [swap(d_head_pieces[k], "seq", k) for k in range(1, seqs)]
    )
    branch_late, att_late, d_up_late = after((d_branch, token_att, d_up), *d_head_pieces)
    att_all = jnp.concatenate(from_all(att_late, "blk"))
    branch_all = jnp.concatenate(
        [
            lax.dynamic_slice_in_dim(branch_late, blk * out_width, out_width, axis=1),
        ]
        + [
            swap(
                lax.dynamic_slice_in_dim(branch_late, (blk ^ m) * out_width, out_width, axis=1),
                "blk",
                m,
            )
            for m in range(1, blocks)
        ]
    )
    grads_up = jnp.concatenate(
        [dot_tn(normed2_all, d_up_late).astype(BF), dot_tn(att_all, branch_all).astype(BF)], axis=1
    )
    half_up = core_sums(grads_up.reshape(owners, own_rows, hidden_width + out_width), own)

    d_attended = after(d_attended, half_down, half_up)
    back = attend_back(key_counts, queries, log_total, d_attended, kv_blocks, rows)
    own_down = owner_sums(half_down, own)
    own_up = owner_sums(half_up, own)
    d_query, d_kv = back[0], back[1]
    for m in range(1, blocks):
        d_kv = d_kv + swap(back[1 + m], "blk", m).astype(F32)
    d_kv = after(d_kv.astype(BF), own_down)
    d_projected = jnp.concatenate([d_query, d_kv], axis=1)
    d_normed1_parts = dot_nt(d_projected, qkv_full).astype(BF)
    d_normed1 = split_sums(d_normed1_parts, "seq")
    sum_down = chunk_sums(own_down, "seq", seq)

    normed1_late, hidden_late = after((normed1_all, hidden), d_normed1_parts)
    half_qkv = core_sums(
        dot_tn(normed1_late, d_projected).astype(BF).reshape(owners, own_rows, 3 * head_width), own
    )
    outcome = split_sums(dot_nn(hidden_late, full_down), "blk")
    activations = jnp.where(own_valid, middle + outcome + biases[3], 0.0)
    sum_up = chunk_sums(own_up, "seq", seq)
    sum_qkv = chunk_sums(owner_sums(half_qkv, own), "blk", blk)
    d_normed1 = after(d_normed1, sum_down)
    d_inputs, d_gain_one, d_shift_one = norm_back(d_normed1, unit1, inverse1, gains[0])
    grad_tokens = d_middle + d_inputs

    bias_sums = jnp.sum(d_projected.astype(F32), axis=0)
    is_seq = (jnp.arange(seqs) == seq)[:, None]
    is_blk = (jnp.arange(blocks) == blk)[None, :, None]
    up_sums = jnp.sum(d_up.astype(F32), axis=0).reshape(owners, 1, hidden_rows)
    vectors = jnp.concatenate(
        [
            d_gain_one,
            d_gain_two,
            d_shift_one,
            d_shift_two,
            jnp.where(is_seq, bias_sums[None, :head_width], 0.0).reshape(-1),
            jnp.where(is_seq, bias_sums[None, 2 * head_width :], 0.0).reshape(-1),
            jnp.sum(d_branch.astype(F32), axis=0),
            jnp.sum(d_outcome.astype(F32), axis=0),
            jnp.where(is_blk, up_sums, 0.0).reshape(-1),
        ]
    ).reshape(-1, 128)
    vectors = sum_over(vectors, ("fsdp", "seq", "blk")).reshape(-1)
    mine = lax.dynamic_slice_in_dim(
        vectors[: 8 * width].reshape(8, width), own * own_rows, own_rows, axis=1
    )
    up_total = lax.dynamic_slice_in_dim(
        vectors[8 * width :], own * blocks * hidden_rows, blocks * hidden_rows
    )

    def spread(array):
        over_seq = from_all(array, "seq")
        over_blk = from_all(jnp.stack(over_seq), "blk")
        return [[piece[k] for k in range(seqs)] for piece in over_blk]

    chunk, seq_rows, blk_rows = hidden_rows // seqs, own_rows // seqs, own_rows // blocks
    (grad_down,) = put_in_place(
        spread(sum_down),
        blk,
        seq,
        [(blocks * hidden_rows, width)],
        [lambda b, k: [(0, width, b * hidden_rows + k * chunk, 0)]],
        "place_down",
    )
    grad_up, grad_w_out = put_in_place(
        spread(sum_up),
        blk,
        seq,
        [(own_rows, blocks * hidden_width), (own_rows, width)],
        [
            lambda b, k: [
                (i * hidden_rows, hidden_rows, k * seq_rows, (i * blocks + b) * hidden_rows)
                for i in range(owners)
            ],
            lambda b, k: [(hidden_width, out_width, k * seq_rows, b * out_width)],
        ],
        "place_up",
    )
    (grad_qkv,) = put_in_place(
        spread(sum_qkv),
        blk,
        seq,
        [(own_rows, 3 * width)],
        [
            lambda b, k: [
                (i * head_width, head_width, b * blk_rows, i * width + k * head_width)
                for i in range(3)
            ]
        ],
        "place_qkv",
    )
    return (
        activations[None],
        grad_tokens[None],
        mine[0:2],
        mine[2:4],
        mine[4:8],
        up_total,
        grad_qkv,
        grad_w_out,
        grad_up,
        grad_down,
    )


def solution(mesh):
    rows = P("fsdp", ("blk", "seq"), None)
    split = P("fsdp", None)
    return jax.shard_map(
        shards,
        mesh=mesh,
        in_specs=(rows, split, P(), P(), P(), P(), split, split, split, split, rows),
        out_specs=(
            rows,
            rows,
            P(None, "fsdp"),
            P(None, "fsdp"),
            P(None, "fsdp"),
            P("fsdp"),
            split,
            split,
            split,
            split,
        ),
        check_vma=False,
    )
```

profile of v0, /device:TPU:0, one launch (start us, length us, event | category | flops | bytes accessed | tf_op | source)
XLA Modules:
  0.0 265.6 jit_solution(6756944059754709709)
XLA Ops:
  12.9 5.1 %collective-permute-start.2 = (bf16[128,768]{1,0:T(8,128)(2,1)S(1)}, bf16[128,768]{1,0:T(8,128)(2,1)}, u32[]{:S(2)}, u32[]{:S(2)}) collective-permute-start(bf16[128,768]{1,0:T(8,128)(2,1)S(1)} %add_convert_fusion.2), channel_id=1, source_target_pairs={{0,3},{1,2},{2,1},{3,0},{4,7},{5,6},{6,5},{7,4},{8,11},{9,10},{10,... | collective-permute-start | bytes 589832 | tf_op jit(solution)/shard_map/ppermute | solution.py:38
  26.6 7.0 %collective-permute-done.3 = bf16[192,576]{1,0:T(8,128)(2,1)} collective-permute-done((bf16[192,576]{1,0:T(8,128)(2,1)S(1)}, bf16[192,576]{1,0:T(8,128)(2,1)}, u32[]{:S(2)}, u32[]{:S(2)}) %collective-permute-start.3) | collective-permute-done | bytes 221216 | tf_op jit(solution)/shard_map/ppermute | solution.py:38
  41.1 5.3 %stack.63.counts_ref = s32[8]{0:T(128)S(1)} concatenate(s32[1]{0:T(128)} %bitcast.2, s32[1]{0:T(128)} %bitcast.3, s32[1]{0:T(128)} %bitcast.4, s32[1]{0:T(128)} %bitcast.5, s32[1]{0:T(128)} %bitcast.6, s32[1]{0:T(128)} %bitcast.7, s32[1]{0:T(128)} %bitcast.8, s32[1]{0:T(128)} %bitcast.9), dimensions={0} | concatenate | bytes 64 | tf_op jit(solution)/shard_map/stack | solution.py:345
  47.9 5.7 %collective-permute-done.12 = bf16[384,768]{1,0:T(8,128)(2,1)} collective-permute-done((bf16[384,768]{1,0:T(8,128)(2,1)}, bf16[384,768]{1,0:T(8,128)(2,1)}, u32[]{:S(2)}, u32[]{:S(2)}) %collective-permute-start.12) | collective-permute-done | bytes 589856 | tf_op jit(solution)/shard_map/ppermute | solution.py:38
  53.6 3.9 %attend.1 = (bf16[512,192]{1,0:T(8,128)(2,1)S(1)}, f32[3,512]{1,0:T(4,128)S(1)}) custom-call(s32[8]{0:T(128)S(1)} %stack.63.counts_ref, bf16[512,192]{1,0:T(8,128)(2,1)S(1)} %fusion.7.q_ref, bf16[512,384]{1,0:T(8,128)(2,1)S(1)} %fusion.6.refs_0_, bf16[512,384]{1,0:T(8,128)(2,1)S(1)} %collective-permute-done.6.refs_1_), custom_call_target="tpu_custom_call" | custom-call | flops 402653184 | bytes 1179648 | tf_op jit(solution)/shard_map/attend/pallas_call | solution.py:114
  57.5 3.6 %collective-permute-start.7 = (bf16[128,192]{1,0:T(8,128)(2,1)S(1)}, bf16[128,192]{1,0:T(8,128)(2,1)S(1)}, u32[]{:S(2)}, u32[]{:S(2)}) collective-permute-start(bf16[128,192]{1,0:T(8,128)(2,1)S(1)} %get-tuple-element.114), channel_id=1, source_target_pairs={{0,3},{1,2},{2,1},{3,0},{4,7},{5,6},{6,5},{7,4},{8,11},{9,10},{10,... | collective-permute-start | bytes 147464 | tf_op jit(solution)/shard_map/ppermute | solution.py:38
  64.4 2.6 collective-permute-done.8
  67.2 3.2 %select_select_fusion.3 = (bf16[384,768]{1,0:T(8,128)(2,1)S(1)}, bf16[384,768]{1,0:T(8,128)(2,1)}, bf16[384,768]{1,0:T(8,128)(2,1)}, bf16[384,768]{1,0:T(8,128)(2,1)}) fusion(bf16[384,768]{1,0:T(8,128)(2,1)S(1)} %collective-permute-done.13, bf16[384,768]{1,0:T(8,128)(2,1)} %collective-permute-done.12, bf16[384,768]{1,0:T(8,128)(2,1)} %collective-permute-done.14, ...), kind=kLoop, calls=%fused_computation.50 | loop fusion | flops 3538944 | bytes 4718599 | tf_op jit(solution)/shard_map/jit(_where)/select_n | solution.py:235
  76.4 3.1 %collective-permute-done.10 = bf16[128,768]{1,0:T(8,128)(2,1)S(1)} collective-permute-done((bf16[128,768]{1,0:T(8,128)(2,1)S(1)}, bf16[128,768]{1,0:T(8,128)(2,1)S(1)}, u32[]{:S(2)}, u32[]{:S(2)}) %collective-permute-start.10) | collective-permute-done | bytes 196640 | tf_op jit(solution)/shard_map/ppermute | solution.py:38
  80.3 3.7 %convert_reduce_fusion = (f32[1536]{0:T(1024)S(1)}, bf16[256,1536]{1,0:T(8,128)(2,1)S(1)}, bf16[256,1536]{1,0:T(8,128)(2,1)S(1)}) fusion(f32[256,1536]{1,0:T(8,128)} %fusion.11, f32[1536]{0:T(1024)S(1)} %maximum_convert_fusion, bf16[256,768]{1,0:T(8,128)(2,1)} %pad_maximum_fusion.11, bf16[768,1536]{1,0:T(8,128)(2,1)} %all-gather.5.cloned.1.call-done), kind=kOutput, calls=%fused_computation.14 | convolution fusion | flops 609876480 | bytes 5910528 | tf_op jit(solution)/shard_map/dot_general | solution.py:20
  87.8 3.0 %collective-permute-done.15 = bf16[128,768]{1,0:T(8,128)(2,1)S(1)} collective-permute-done((bf16[128,768]{1,0:T(8,128)(2,1)S(1)}, bf16[128,768]{1,0:T(8,128)(2,1)S(1)}, u32[]{:S(2)}, u32[]{:S(2)}) %collective-permute-start.15) | collective-permute-done | bytes 196640 | tf_op jit(solution)/shard_map/ppermute | solution.py:38
  97.2 4.2 %collective-permute-done.21 = bf16[128,384]{1,0:T(8,128)(2,1)S(1)} collective-permute-done((bf16[128,384]{1,0:T(8,128)(2,1)S(1)}, bf16[128,384]{1,0:T(8,128)(2,1)S(1)}, u32[]{:S(2)}, u32[]{:S(2)}) %collective-permute-start.21) | collective-permute-done | bytes 98336 | tf_op jit(solution)/shard_map/ppermute | solution.py:38
  113.5 2.6 collective-permute-done.17
  117.1 3.8 %collective-permute-done.28 = bf16[1,384,768]{2,1,0:T(8,128)(2,1)} collective-permute-done((bf16[1,384,768]{2,1,0:T(8,128)(2,1)S(1)}, bf16[1,384,768]{2,1,0:T(8,128)(2,1)}, u32[]{:S(2)}, u32[]{:S(2)}) %collective-permute-start.28) | collective-permute-done | bytes 589856 | tf_op jit(solution)/shard_map/ppermute | solution.py:38
  128.6 5.6 %attend_back.1 = (bf16[512,192]{1,0:T(8,128)(2,1)S(1)}, f32[512,384]{1,0:T(8,128)S(1)}, bf16[512,384]{1,0:T(8,128)(2,1)S(1)}) custom-call(s32[8]{0:T(128)S(1)} %stack.63.counts_ref, bf16[512,192]{1,0:T(8,128)(2,1)S(1)} %fusion.7.q_ref, f32[3,512]{1,0:T(4,128)S(1)} %get-tuple-element.38.log_ref, bf16[512,192]{1,0:T(8,128)(2,1)S(1)} %pad_maximum_fusion.13.d_ref, ...), custom_call_target="tpu_custom_call" | custom-call | flops 1006632960 | bytes 2555904 | tf_op jit(solution)/shard_map/attend_back/pallas_call | solution.py:137
  139.1 2.6 collective-permute-start.54
  143.6 7.0 %collective-permute-done.53.refs_2_ = bf16[96,768]{1,0:T(8,128)(2,1)S(1)} collective-permute-done((bf16[96,768]{1,0:T(8,128)(2,1)S(1)}, bf16[96,768]{1,0:T(8,128)(2,1)S(1)}, u32[]{:S(2)}, u32[]{:S(2)}) %collective-permute-start.53) | collective-permute-done | bytes 147488 | tf_op jit(solution)/shard_map/ppermute | solution.py:38
  164.4 2.7 %collective-permute-done.27 = bf16[128,768]{1,0:T(8,128)(2,1)} collective-permute-done((bf16[128,768]{1,0:T(8,128)(2,1)S(1)}, bf16[128,768]{1,0:T(8,128)(2,1)}, u32[]{:S(2)}, u32[]{:S(2)}) %collective-permute-start.27) | collective-permute-done | bytes 196640 | tf_op jit(solution)/shard_map/ppermute | solution.py:38
  167.3 7.3 %collective-permute-done.26 = bf16[128,768]{1,0:T(8,128)(2,1)} collective-permute-done((bf16[128,768]{1,0:T(8,128)(2,1)}, bf16[128,768]{1,0:T(8,128)(2,1)}, u32[]{:S(2)}, u32[]{:S(2)}) %collective-permute-start.26) | collective-permute-done | bytes 196640 | tf_op jit(solution)/shard_map/ppermute | solution.py:38
  179.4 2.4 collective-permute-done.33
  182.8 3.1 %collective-permute-done.34 = f32[72,128]{1,0:T(8,128)S(1)} collective-permute-done((f32[72,128]{1,0:T(8,128)S(1)}, f32[72,128]{1,0:T(8,128)S(1)}, u32[]{:S(2)}, u32[]{:S(2)}) %collective-permute-start.34) | collective-permute-done | bytes 36896 | tf_op jit(solution)/shard_map/ppermute | solution.py:38
  187.6 3.2 %collective-permute-done.35 = f32[72,128]{1,0:T(8,128)S(1)} collective-permute-done((f32[72,128]{1,0:T(8,128)S(1)}, f32[72,128]{1,0:T(8,128)S(1)}, u32[]{:S(2)}, u32[]{:S(2)}) %collective-permute-start.35) | collective-permute-done | bytes 36896 | tf_op jit(solution)/shard_map/ppermute | solution.py:38
  201.5 5.7 %collective-permute-done.46 = bf16[48,1920]{1,0:T(8,128)(2,1)S(1)} collective-permute-done((bf16[48,1920]{1,0:T(8,128)(2,1)S(1)}, bf16[48,1920]{1,0:T(8,128)(2,1)S(1)}, u32[]{:S(2)}, u32[]{:S(2)}) %collective-permute-start.46) | collective-permute-done | bytes 184352 | tf_op jit(solution)/shard_map/ppermute | solution.py:38
  207.4 2.5 collective-permute-start.49
  211.9 6.1 %collective-permute-done.48.refs_1_ = bf16[48,1920]{1,0:T(8,128)(2,1)S(1)} collective-permute-done((bf16[48,1920]{1,0:T(8,128)(2,1)S(1)}, bf16[48,1920]{1,0:T(8,128)(2,1)S(1)}, u32[]{:S(2)}, u32[]{:S(2)}) %collective-permute-start.48) | collective-permute-done | bytes 184352 | tf_op jit(solution)/shard_map/ppermute | solution.py:38
  218.0 7.0 %collective-permute-done.49.refs_2_ = bf16[48,1920]{1,0:T(8,128)(2,1)S(1)} collective-permute-done((bf16[48,1920]{1,0:T(8,128)(2,1)S(1)}, bf16[48,1920]{1,0:T(8,128)(2,1)S(1)}, u32[]{:S(2)}, u32[]{:S(2)}) %collective-permute-start.49) | collective-permute-done | bytes 184352 | tf_op jit(solution)/shard_map/ppermute | solution.py:38
  227.0 2.8 %collective-permute-start.51 = (bf16[4,48,1920]{2,1,0:T(8,128)(2,1)S(1)}, bf16[4,48,1920]{2,1,0:T(8,128)(2,1)S(1)}, u32[]{:S(2)}, u32[]{:S(2)}) collective-permute-start(bf16[4,48,1920]{2,1,0:T(8,128)(2,1)S(1)} %pad_maximum_fusion.4), channel_id=1, source_target_pairs={{0,4},{4,0},{1,5},{5,1},{2,6},{6,2},{3,7},{7,3},{8,12},{12,8},{9,1... | collective-permute-start | bytes 2211848 | tf_op jit(solution)/shard_map/ppermute | solution.py:38
  229.8 3.9 %collective-permute-done.41.refs_2_ = bf16[96,576]{1,0:T(8,128)(2,1)S(1)} collective-permute-done((bf16[96,576]{1,0:T(8,128)(2,1)S(1)}, bf16[96,576]{1,0:T(8,128)(2,1)S(1)}, u32[]{:S(2)}, u32[]{:S(2)}) %collective-permute-start.41) | collective-permute-done | bytes 110624 | tf_op jit(solution)/shard_map/ppermute | solution.py:38
  239.1 3.7 %place_down.1 = f32[768,768]{1,0:T(8,128)} custom-call(s32[2]{0:T(128)S(1)} %pad_add_fusion.place_ref, bf16[96,768]{1,0:T(8,128)(2,1)S(1)} %fusion.36.refs_0_, bf16[96,768]{1,0:T(8,128)(2,1)S(1)} %collective-permute-done.52.refs_1_, bf16[96,768]{1,0:T(8,128)(2,1)S(1)} %collective-permute-done.53.refs_2_, ...), custom_call_target="tpu_custom_call" | custom-call | bytes 3538944 | tf_op jit(solution)/shard_map/place_down/pallas_call | solution.py:269
  242.8 7.1 %collective-permute-done.43 = bf16[4,96,576]{2,1,0:T(8,128)(2,1)} collective-permute-done((bf16[4,96,576]{2,1,0:T(8,128)(2,1)}, bf16[4,96,576]{2,1,0:T(8,128)(2,1)}, u32[]{:S(2)}, u32[]{:S(2)}) %collective-permute-start.43) | collective-permute-done | bytes 442400 | tf_op jit(solution)/shard_map/ppermute | solution.py:38
  251.0 3.3 %place_qkv.1 = f32[192,2304]{1,0:T(8,128)} custom-call(s32[2]{0:T(128)S(1)} %pad_add_fusion.place_ref, bf16[96,576]{1,0:T(8,128)(2,1)S(1)} %fusion.41.refs_0_, bf16[96,576]{1,0:T(8,128)(2,1)S(1)} %collective-permute-done.40.refs_1_, bf16[96,576]{1,0:T(8,128)(2,1)S(1)} %collective-permute-done.41.refs_2_, ...), custom_call_target="tpu_custom_call" | custom-call | bytes 2654208 | tf_op jit(solution)/shard_map/place_qkv/pallas_call | solution.py:269
  254.4 4.3 %place_up.1 = (f32[192,3072]{1,0:T(8,128)}, f32[192,768]{1,0:T(8,128)}) custom-call(s32[2]{0:T(128)S(1)} %pad_add_fusion.place_ref, bf16[48,1920]{1,0:T(8,128)(2,1)S(1)} %fusion.30.refs_0_, bf16[48,1920]{1,0:T(8,128)(2,1)S(1)} %collective-permute-done.48.refs_1_, bf16[48,1920]{1,0:T(8,128)(2,1)S(1)} %collective-permute-done.49.refs_2_, ...), custom_call_target="tpu_custom_call" | custom-call | bytes 4423680 | tf_op jit(solution)/shard_map/place_up/pallas_call | solution.py:269
  (331 shorter events, 113.3 us)
Async XLA Ops:
  7.2 63.2 %all-gather.3.cloned.1.call-start = ((), (), s32[]{:S(2)}) async-start(), calls=%async_computation | async-start | bytes 1474560 | tf_op jit(solution)/shard_map/all_gather | solution.py:316
  7.9 72.4 %all-gather.5.cloned.1.call-start = ((), (), s32[]{:S(2)}) async-start(), calls=%async_computation.1 | async-start | bytes 2949120 | tf_op jit(solution)/shard_map/all_gather | solution.py:327
  12.9 24.1 %collective-permute-start.2 = (bf16[128,768]{1,0:T(8,128)(2,1)S(1)}, bf16[128,768]{1,0:T(8,128)(2,1)}, u32[]{:S(2)}, u32[]{:S(2)}) collective-permute-start(bf16[128,768]{1,0:T(8,128)(2,1)S(1)} %add_convert_fusion.2), channel_id=1, source_target_pairs={{0,3},{1,2},{2,1},{3,0},{4,7},{5,6},{6,5},{7,4},{8,11},{9,10},{10,... | collective-permute-start | bytes 589832 | tf_op jit(solution)/shard_map/ppermute | solution.py:38
  18.0 20.7 %collective-permute-start.1 = (bf16[128,768]{1,0:T(8,128)(2,1)S(1)}, bf16[128,768]{1,0:T(8,128)(2,1)}, u32[]{:S(2)}, u32[]{:S(2)}) collective-permute-start(bf16[128,768]{1,0:T(8,128)(2,1)S(1)} %add_convert_fusion.2), channel_id=1, source_target_pairs={{0,2},{1,3},{2,0},{3,1},{4,6},{5,7},{6,4},{7,5},{8,10},{9,11},{10,... | collective-permute-start | bytes 589832 | tf_op jit(solution)/shard_map/ppermute | solution.py:38
  18.0 20.7 %collective-permute-start = (bf16[128,768]{1,0:T(8,128)(2,1)S(1)}, bf16[128,768]{1,0:T(8,128)(2,1)}, u32[]{:S(2)}, u32[]{:S(2)}) collective-permute-start(bf16[128,768]{1,0:T(8,128)(2,1)S(1)} %add_convert_fusion.2), channel_id=1, source_target_pairs={{0,1},{1,0},{2,3},{3,2},{4,5},{5,4},{6,7},{7,6},{8,9},{9,8},{10,11... | collective-permute-start | bytes 589832 | tf_op jit(solution)/shard_map/ppermute | solution.py:38
  20.0 13.5 %collective-permute-start.3 = (bf16[192,576]{1,0:T(8,128)(2,1)S(1)}, bf16[192,576]{1,0:T(8,128)(2,1)}, u32[]{:S(2)}, u32[]{:S(2)}) collective-permute-start(bf16[192,576]{1,0:T(8,128)(2,1)S(1)} %pad_maximum_fusion.14), channel_id=1, source_target_pairs={{0,16},{8,24},{16,0},{24,8},{1,17},{9,25},{17,1},{25,9},{2,18},{10... | collective-permute-start | bytes 663560 | tf_op jit(solution)/shard_map/ppermute | solution.py:38
  34.3 19.4 %collective-permute-start.12 = (bf16[384,768]{1,0:T(8,128)(2,1)}, bf16[384,768]{1,0:T(8,128)(2,1)}, u32[]{:S(2)}, u32[]{:S(2)}) collective-permute-start(bf16[384,768]{1,0:T(8,128)(2,1)} %constant_dynamic-slice_fusion.7), channel_id=1, source_target_pairs={{0,16},{8,24},{16,0},{24,8},{1,17},{9,25},{17,1},{25,9},{2,18},{10... | collective-permute-start | bytes 1769480 | tf_op jit(solution)/shard_map/ppermute | solution.py:38
  35.3 31.9 %collective-permute-start.14 = (bf16[384,768]{1,0:T(8,128)(2,1)}, bf16[384,768]{1,0:T(8,128)(2,1)}, u32[]{:S(2)}, u32[]{:S(2)}) collective-permute-start(bf16[384,768]{1,0:T(8,128)(2,1)} %constant_dynamic-slice_fusion.7), channel_id=1, source_target_pairs={{0,8},{8,0},{16,24},{24,16},{1,9},{9,1},{17,25},{25,17},{2,10},{10... | collective-permute-start | bytes 1769480 | tf_op jit(solution)/shard_map/ppermute | solution.py:38
  37.0 24.2 %collective-permute-start.11 = (bf16[128,768]{1,0:T(8,128)(2,1)S(1)}, bf16[128,768]{1,0:T(8,128)(2,1)S(1)}, u32[]{:S(2)}, u32[]{:S(2)}) collective-permute-start(bf16[128,768]{1,0:T(8,128)(2,1)S(1)} %get-tuple-element.69), channel_id=1, source_target_pairs={{0,4},{4,0},{1,5},{5,1},{2,6},{6,2},{3,7},{7,3},{8,12},{12,8},{9,1... | collective-permute-start | bytes 589832 | tf_op jit(solution)/shard_map/ppermute | solution.py:38
  40.4 13.2 %collective-permute-start.6 = (bf16[512,384]{1,0:T(8,128)(2,1)S(1)}, bf16[512,384]{1,0:T(8,128)(2,1)S(1)}, u32[]{:S(2)}, u32[]{:S(2)}) collective-permute-start(bf16[512,384]{1,0:T(8,128)(2,1)S(1)} %fusion.6.refs_0_), channel_id=1, source_target_pairs={{0,4},{4,0},{1,5},{5,1},{2,6},{6,2},{3,7},{7,3},{8,12},{12,8},{9,1... | collective-permute-start | bytes 1179656 | tf_op jit(solution)/shard_map/ppermute | solution.py:38
  53.6 13.6 %collective-permute-start.13 = (bf16[384,768]{1,0:T(8,128)(2,1)}, bf16[384,768]{1,0:T(8,128)(2,1)S(1)}, u32[]{:S(2)}, u32[]{:S(2)}) collective-permute-start(bf16[384,768]{1,0:T(8,128)(2,1)} %collective-permute-done.12), channel_id=1, source_target_pairs={{0,8},{8,0},{16,24},{24,16},{1,9},{9,1},{17,25},{25,17},{2,10},{10... | collective-permute-start | bytes 1769480 | tf_op jit(solution)/shard_map/ppermute | solution.py:38
  87.7 15.6 %collective-permute-start.19 = (bf16[2,384,768]{2,1,0:T(8,128)(2,1)S(1)}, bf16[2,384,768]{2,1,0:T(8,128)(2,1)S(1)}, u32[]{:S(2)}, u32[]{:S(2)}) collective-permute-start(bf16[2,384,768]{2,1,0:T(8,128)(2,1)S(1)} %dynamic-slice_bitcast_fusion.1), channel_id=1, source_target_pairs={{0,8},{8,0},{16,24},{24,16},{1,9},{9,1},{17,25},{25,17},{2,10},{10... | collective-permute-start | bytes 3538952 | tf_op jit(solution)/shard_map/ppermute | solution.py:38
  103.3 23.6 %collective-permute-start.22 = (bf16[2,192,1920]{2,1,0:T(8,128)(2,1)}, bf16[2,192,1920]{2,1,0:T(8,128)(2,1)}, u32[]{:S(2)}, u32[]{:S(2)}) collective-permute-start(bf16[2,192,1920]{2,1,0:T(8,128)(2,1)} %dynamic-slice_bitcast_fusion), channel_id=1, source_target_pairs={{0,8},{8,0},{16,24},{24,16},{1,9},{9,1},{17,25},{25,17},{2,10},{10... | collective-permute-start | bytes 4423688 | tf_op jit(solution)/shard_map/ppermute | solution.py:38
  105.5 15.4 %collective-permute-start.28 = (bf16[1,384,768]{2,1,0:T(8,128)(2,1)S(1)}, bf16[1,384,768]{2,1,0:T(8,128)(2,1)}, u32[]{:S(2)}, u32[]{:S(2)}) collective-permute-start(bf16[1,384,768]{2,1,0:T(8,128)(2,1)S(1)} %dynamic-slice_convert_fusion.1), channel_id=1, source_target_pairs={{0,16},{8,24},{16,0},{24,8},{1,17},{9,25},{17,1},{25,9},{2,18},{10... | collective-permute-start | bytes 1769480 | tf_op jit(solution)/shard_map/ppermute | solution.py:38
  122.5 13.6 %collective-permute-start.31 = (bf16[96,768]{1,0:T(8,128)(2,1)S(1)}, bf16[96,768]{1,0:T(8,128)(2,1)S(1)}, u32[]{:S(2)}, u32[]{:S(2)}) collective-permute-start(bf16[96,768]{1,0:T(8,128)(2,1)S(1)} %get-tuple-element.82), channel_id=1, source_target_pairs={{0,3},{1,2},{2,1},{3,0},{4,7},{5,6},{6,5},{7,4},{8,11},{9,10},{10,... | collective-permute-start | bytes 442376 | tf_op jit(solution)/shard_map/ppermute | solution.py:38
  124.6 12.5 %collective-permute-start.30 = (bf16[96,768]{1,0:T(8,128)(2,1)S(1)}, bf16[96,768]{1,0:T(8,128)(2,1)S(1)}, u32[]{:S(2)}, u32[]{:S(2)}) collective-permute-start(bf16[96,768]{1,0:T(8,128)(2,1)S(1)} %get-tuple-element.83), channel_id=1, source_target_pairs={{0,2},{1,3},{2,0},{3,1},{4,6},{5,7},{6,4},{7,5},{8,10},{9,11},{10,... | collective-permute-start | bytes 442376 | tf_op jit(solution)/shard_map/ppermute | solution.py:38
  134.2 19.0 %collective-permute-start.23 = (bf16[512,384]{1,0:T(8,128)(2,1)S(1)}, bf16[512,384]{1,0:T(8,128)(2,1)S(1)}, u32[]{:S(2)}, u32[]{:S(2)}) collective-permute-start(bf16[512,384]{1,0:T(8,128)(2,1)S(1)} %get-tuple-element.46), channel_id=1, source_target_pairs={{0,4},{4,0},{1,5},{5,1},{2,6},{6,2},{3,7},{7,3},{8,12},{12,8},{9,1... | collective-permute-start | bytes 1179656 | tf_op jit(solution)/shard_map/ppermute | solution.py:38
  137.3 13.3 %collective-permute-start.53 = (bf16[96,768]{1,0:T(8,128)(2,1)S(1)}, bf16[96,768]{1,0:T(8,128)(2,1)S(1)}, u32[]{:S(2)}, u32[]{:S(2)}) collective-permute-start(bf16[96,768]{1,0:T(8,128)(2,1)S(1)} %fusion.36.refs_0_), channel_id=1, source_target_pairs={{0,2},{1,3},{2,0},{3,1},{4,6},{5,7},{6,4},{7,5},{8,10},{9,11},{10,... | collective-permute-start | bytes 442376 | tf_op jit(solution)/shard_map/ppermute | solution.py:38
  142.7 43.6 %collective-permute-start.44 = (bf16[1,192,1920]{2,1,0:T(8,128)(2,1)}, bf16[1,192,1920]{2,1,0:T(8,128)(2,1)}, u32[]{:S(2)}, u32[]{:S(2)}) collective-permute-start(bf16[1,192,1920]{2,1,0:T(8,128)(2,1)} %dynamic-slice_convert_fusion), channel_id=1, source_target_pairs={{0,16},{8,24},{16,0},{24,8},{1,17},{9,25},{17,1},{25,9},{2,18},{10... | collective-permute-start | bytes 2211848 | tf_op jit(solution)/shard_map/ppermute | solution.py:38
  151.5 86.4 %collective-permute-start.55 = (bf16[4,96,768]{2,1,0:T(8,128)(2,1)}, bf16[4,96,768]{2,1,0:T(8,128)(2,1)}, u32[]{:S(2)}, u32[]{:S(2)}) collective-permute-start(bf16[4,96,768]{2,1,0:T(8,128)(2,1)} %pad_maximum_fusion.7), channel_id=1, source_target_pairs={{0,4},{4,0},{1,5},{5,1},{2,6},{6,2},{3,7},{7,3},{8,12},{12,8},{9,1... | collective-permute-start | bytes 1769480 | tf_op jit(solution)/shard_map/ppermute | solution.py:38
  158.9 15.8 %collective-permute-start.26 = (bf16[128,768]{1,0:T(8,128)(2,1)}, bf16[128,768]{1,0:T(8,128)(2,1)}, u32[]{:S(2)}, u32[]{:S(2)}) collective-permute-start(bf16[128,768]{1,0:T(8,128)(2,1)} %get-tuple-element.97), channel_id=1, source_target_pairs={{0,2},{1,3},{2,0},{3,1},{4,6},{5,7},{6,4},{7,5},{8,10},{9,11},{10,... | collective-permute-start | bytes 589832 | tf_op jit(solution)/shard_map/ppermute | solution.py:38
  161.0 13.7 %collective-permute-start.25 = (bf16[128,768]{1,0:T(8,128)(2,1)}, bf16[128,768]{1,0:T(8,128)(2,1)}, u32[]{:S(2)}, u32[]{:S(2)}) collective-permute-start(bf16[128,768]{1,0:T(8,128)(2,1)} %get-tuple-element.95), channel_id=1, source_target_pairs={{0,1},{1,0},{2,3},{3,2},{4,5},{5,4},{6,7},{7,6},{8,9},{9,8},{10,11... | collective-permute-start | bytes 589832 | tf_op jit(solution)/shard_map/ppermute | solution.py:38
  167.1 14.8 %collective-permute-start.24 = (bf16[128,768]{1,0:T(8,128)(2,1)}, bf16[128,768]{1,0:T(8,128)(2,1)S(1)}, u32[]{:S(2)}, u32[]{:S(2)}) collective-permute-start(bf16[128,768]{1,0:T(8,128)(2,1)} %slice.244), channel_id=1, source_target_pairs={{0,4},{4,0},{1,5},{5,1},{2,6},{6,2},{3,7},{7,3},{8,12},{12,8},{9,1... | collective-permute-start | bytes 589832 | tf_op jit(solution)/shard_map/ppermute | solution.py:38
  174.6 16.9 %collective-permute-start.37 = (bf16[2,192,576]{2,1,0:T(8,128)(2,1)S(1)}, bf16[2,192,576]{2,1,0:T(8,128)(2,1)S(1)}, u32[]{:S(2)}, u32[]{:S(2)}) collective-permute-start(bf16[2,192,576]{2,1,0:T(8,128)(2,1)S(1)} %dynamic-slice_bitcast_fusion.2), channel_id=1, source_target_pairs={{0,8},{8,0},{16,24},{24,16},{1,9},{9,1},{17,25},{25,17},{2,10},{10... | collective-permute-start | bytes 1327112 | tf_op jit(solution)/shard_map/ppermute | solution.py:38
  194.4 12.8 %collective-permute-start.46 = (bf16[48,1920]{1,0:T(8,128)(2,1)S(1)}, bf16[48,1920]{1,0:T(8,128)(2,1)S(1)}, u32[]{:S(2)}, u32[]{:S(2)}) collective-permute-start(bf16[48,1920]{1,0:T(8,128)(2,1)S(1)} %get-tuple-element.80), channel_id=1, source_target_pairs={{0,2},{1,3},{2,0},{3,1},{4,6},{5,7},{6,4},{7,5},{8,10},{9,11},{10,... | collective-permute-start | bytes 552968 | tf_op jit(solution)/shard_map/ppermute | solution.py:38
  198.1 13.7 %collective-permute-start.39 = (bf16[96,576]{1,0:T(8,128)(2,1)S(1)}, bf16[96,576]{1,0:T(8,128)(2,1)S(1)}, u32[]{:S(2)}, u32[]{:S(2)}) collective-permute-start(bf16[96,576]{1,0:T(8,128)(2,1)S(1)} %fusion.51), channel_id=1, source_target_pairs={{0,4},{4,0},{1,5},{5,1},{2,6},{6,2},{3,7},{7,3},{8,12},{12,8},{9,1... | collective-permute-start | bytes 331784 | tf_op jit(solution)/shard_map/ppermute | solution.py:38
  207.4 17.6 %collective-permute-start.49 = (bf16[48,1920]{1,0:T(8,128)(2,1)S(1)}, bf16[48,1920]{1,0:T(8,128)(2,1)S(1)}, u32[]{:S(2)}, u32[]{:S(2)}) collective-permute-start(bf16[48,1920]{1,0:T(8,128)(2,1)S(1)} %fusion.30.refs_0_), channel_id=1, source_target_pairs={{0,2},{1,3},{2,0},{3,1},{4,6},{5,7},{6,4},{7,5},{8,10},{9,11},{10,... | collective-permute-start | bytes 552968 | tf_op jit(solution)/shard_map/ppermute | solution.py:38
  209.9 17.0 %collective-permute-start.50 = (bf16[48,1920]{1,0:T(8,128)(2,1)S(1)}, bf16[48,1920]{1,0:T(8,128)(2,1)S(1)}, u32[]{:S(2)}, u32[]{:S(2)}) collective-permute-start(bf16[48,1920]{1,0:T(8,128)(2,1)S(1)} %fusion.30.refs_0_), channel_id=1, source_target_pairs={{0,3},{1,2},{2,1},{3,0},{4,7},{5,6},{6,5},{7,4},{8,11},{9,10},{10,... | collective-permute-start | bytes 552968 | tf_op jit(solution)/shard_map/ppermute | solution.py:38
  211.8 18.0 %collective-permute-start.40 = (bf16[96,576]{1,0:T(8,128)(2,1)S(1)}, bf16[96,576]{1,0:T(8,128)(2,1)S(1)}, u32[]{:S(2)}, u32[]{:S(2)}) collective-permute-start(bf16[96,576]{1,0:T(8,128)(2,1)S(1)} %fusion.41.refs_0_), channel_id=1, source_target_pairs={{0,1},{1,0},{2,3},{3,2},{4,5},{5,4},{6,7},{7,6},{8,9},{9,8},{10,11... | collective-permute-start | bytes 331784 | tf_op jit(solution)/shard_map/ppermute | solution.py:38
  218.0 15.8 %collective-permute-start.41 = (bf16[96,576]{1,0:T(8,128)(2,1)S(1)}, bf16[96,576]{1,0:T(8,128)(2,1)S(1)}, u32[]{:S(2)}, u32[]{:S(2)}) collective-permute-start(bf16[96,576]{1,0:T(8,128)(2,1)S(1)} %fusion.41.refs_0_), channel_id=1, source_target_pairs={{0,2},{1,3},{2,0},{3,1},{4,6},{5,7},{6,4},{7,5},{8,10},{9,11},{10,... | collective-permute-start | bytes 331784 | tf_op jit(solution)/shard_map/ppermute | solution.py:38
  227.0 27.4 %collective-permute-start.51 = (bf16[4,48,1920]{2,1,0:T(8,128)(2,1)S(1)}, bf16[4,48,1920]{2,1,0:T(8,128)(2,1)S(1)}, u32[]{:S(2)}, u32[]{:S(2)}) collective-permute-start(bf16[4,48,1920]{2,1,0:T(8,128)(2,1)S(1)} %pad_maximum_fusion.4), channel_id=1, source_target_pairs={{0,4},{4,0},{1,5},{5,1},{2,6},{6,2},{3,7},{7,3},{8,12},{12,8},{9,1... | collective-permute-start | bytes 2211848 | tf_op jit(solution)/shard_map/ppermute | solution.py:38
  234.6 15.3 %collective-permute-start.43 = (bf16[4,96,576]{2,1,0:T(8,128)(2,1)}, bf16[4,96,576]{2,1,0:T(8,128)(2,1)}, u32[]{:S(2)}, u32[]{:S(2)}) collective-permute-start(bf16[4,96,576]{2,1,0:T(8,128)(2,1)} %pad_maximum_fusion.8), channel_id=1, source_target_pairs={{0,4},{4,0},{1,5},{5,1},{2,6},{6,2},{3,7},{7,3},{8,12},{12,8},{9,1... | collective-permute-start | bytes 1327112 | tf_op jit(solution)/shard_map/ppermute | solution.py:38
  (82 other events, 619.2 us)
Sparse Core Ops, SparseCore 0:
  9.6 25.3 all-gather.2
  37.1 27.1 all-gather.4
where the time goes:
time: 270 us; the launch traced here: 266 us
  waiting for transfers between devices  97 us (36%)
  starting transfers between devices  61.9 us (23%)
  other arithmetic  31.3 us (12%)
  local copies, waits for them, and re-layouts  22.8 us (8%)
  Pallas kernels  20.8 us (8%)
  matrix products  16.5 us (6%)
  between operations  15.4 us (6%)
    ppermute x56, waiting for transfers between devices, swap(): lax.ppermute(array, axis, [(i, i ^ bits) for i in range(lax.axis_size(axi...  96.3 us
    ppermute x56, starting transfers between devices, swap(): lax.ppermute(array, axis, [(i, i ^ bits) for i in range(lax.axis_size(axi...  61.8 us
    pallas_call x3, Pallas kernels, put_in_place(): pl.pallas_call(functools.partial(place_kernel, seqs, blocks, layouts), ou...  11.3 us
    dot_general x5, matrix products, dot_nn(): lax.dot_general(left_side, right_side, (((1,), (0,)), ((), ())), preferre...  8.91 us
    pallas_call x1, Pallas kernels, attend_back(): pl.pallas_call(functools.partial(attend_back_kernel, blocks, heads, piece...  5.63 us
  transfers between devices with their start and end apart: 58, of which 29 were waited for; matrix products, arithmetic and copies ran while one was open for 24% of the time, Pallas kernels for 6%

commit v1 on v0

--- a/solution.py
+++ b/solution.py
@@ -51,19 +51,20 @@
     return [pieces[j] for j in range(lax.axis_size(axis))]
 
 
-def piece_bias(counts_ref, first_piece, pieces, slot_rows):
+def piece_bias(place_ref, counts_ref, block, pieces, slot_rows):
     row = lax.broadcasted_iota(jnp.int32, (pieces * slot_rows, 1), 0)
     limit = jnp.zeros_like(row)
     for piece in range(pieces):
-        end = counts_ref[first_piece + piece] + piece * slot_rows
+        held = (place_ref[0] ^ block) * pieces + (place_ref[1] ^ piece)
+        end = counts_ref[0, held] + piece * slot_rows
         limit = jnp.where(row >= piece * slot_rows, end, limit)
     return jnp.where(row < limit, 0.0, MASKED)
 
 
-def attend_kernel(blocks, heads, pieces, slot_rows, counts_ref, q_ref, *refs):
+def attend_kernel(blocks, heads, pieces, slot_rows, place_ref, counts_ref, q_ref, *refs):
     kv_refs, (out_ref, log_ref) = refs[:blocks], refs[blocks:]
     width = heads * HD
-    biases = [piece_bias(counts_ref, m * pieces, pieces, slot_rows) for m in range(blocks)]
+    biases = [piece_bias(place_ref, counts_ref, m, pieces, slot_rows) for m in range(blocks)]
     for head in range(heads):
         low, high = head * HD, (head + 1) * HD
         query = q_ref[:, low:high] * SCALE
@@ -82,10 +83,12 @@
         log_ref[head : head + 1, :] = top + jnp.log(total)
 
 
-def attend_back_kernel(blocks, heads, pieces, slot_rows, counts_ref, q_ref, log_ref, d_ref, *refs):
+def attend_back_kernel(
+    blocks, heads, pieces, slot_rows, place_ref, counts_ref, q_ref, log_ref, d_ref, *refs
+):
     kv_refs, dq_ref, dkv_refs = refs[:blocks], refs[blocks], refs[blocks + 1 :]
     width = heads * HD
-    biases = [piece_bias(counts_ref, m * pieces, pieces, slot_rows) for m in range(blocks)]
+    biases = [piece_bias(place_ref, counts_ref, m, pieces, slot_rows) for m in range(blocks)]
     for head in range(heads):
         low, high = head * HD, (head + 1) * HD
         query = q_ref[:, low:high] * SCALE
@@ -107,7 +110,7 @@
         dq_ref[:, low:high] = (d_query * SCALE).astype(BF)
 
 
-def attend(counts, queries, kv_blocks, slot_rows):
+def attend(place, counts, queries, kv_blocks, slot_rows):
     rows, width = queries.shape
     blocks, heads = len(kv_blocks), width // HD
     pieces = kv_blocks[0].shape[0] // slot_rows
@@ -117,7 +120,7 @@
             jax.ShapeDtypeStruct((rows, width), BF),
             jax.ShapeDtypeStruct((heads, rows), F32),
         ),
-        in_specs=[pl.BlockSpec(memory_space=pltpu.SMEM)]
+        in_specs=[pl.BlockSpec(memory_space=pltpu.SMEM)] * 2
         + [pl.BlockSpec(memory_space=pltpu.VMEM)] * (1 + blocks),
         out_specs=(pl.BlockSpec(memory_space=pltpu.VMEM),) * 2,
         compiler_params=pltpu.CompilerParams(vmem_limit_bytes=VMEM_LIMIT),
@@ -127,10 +130,10 @@
             transcendentals=rows * rows * blocks * heads,
         ),
         name="attend",
-    )(counts, queries, *kv_blocks)
-
-
-def attend_back(counts, queries, log_total, d_out, kv_blocks, slot_rows):
+    )(place, counts, queries, *kv_blocks)
+
+
+def attend_back(place, counts, queries, log_total, d_out, kv_blocks, slot_rows):
     rows, width = queries.shape
     blocks, heads = len(kv_blocks), width // HD
     pieces = kv_blocks[0].shape[0] // slot_rows
@@ -141,7 +144,7 @@
             jax.ShapeDtypeStruct(block.shape, F32 if m == 0 else BF)
             for m, block in enumerate(kv_blocks)
         ),
-        in_specs=[pl.BlockSpec(memory_space=pltpu.SMEM)]
+        in_specs=[pl.BlockSpec(memory_space=pltpu.SMEM)] * 2
         + [pl.BlockSpec(memory_space=pltpu.VMEM)] * (3 + blocks),
         out_specs=(pl.BlockSpec(memory_space=pltpu.VMEM),) * (1 + blocks),
         compiler_params=pltpu.CompilerParams(vmem_limit_bytes=VMEM_LIMIT),
@@ -151,7 +154,7 @@
             transcendentals=rows * rows * blocks * heads,
         ),
         name="attend_back",
-    )(counts, queries, log_total, d_out, *kv_blocks)
+    )(place, counts, queries, log_total, d_out, *kv_blocks)
 
 
 def normalised(matrix_rows):
@@ -263,7 +266,7 @@
                     out[row : row + piece.shape[0], column : column + size] = piece.astype(F32)
 
 
-def put_in_place(pieces, blk, seq, shapes, layouts, label):
+def put_in_place(pieces, place, shapes, layouts, label):
     blocks, seqs = len(pieces), len(pieces[0])
     piece = pieces[0][0]
     return pl.pallas_call(
@@ -281,7 +284,7 @@
             flops=0, bytes_accessed=6 * blocks * seqs * piece.size, transcendentals=0
         ),
         name=label,
-    )(jnp.stack([blk, seq]), *[one for row in pieces for one in row])
+    )(place, *[one for row in pieces for one in row])
 
 
 def shards(
@@ -313,8 +316,10 @@
     normed1_all = jnp.concatenate(from_all(normed1, "seq"))
     qkv_full = jnp.concatenate(in_order(doubled(qkv_mine, "fsdp"), own))
 
-    full_out = lax.all_gather(w_out, "fsdp", axis=0, tiled=True)
-    up_late, down_late, grad_late = after((w_up, w_down, grad_out), normed1, qkv_mine)
+    up_late, down_late, out_late, grad_late = after(
+        (w_up, w_down, w_out, grad_out), normed1, qkv_mine
+    )
+    full_out = jnp.concatenate(in_order(doubled(out_late, "fsdp"), own))
     up_mine = jnp.concatenate(
         [
             lax.dynamic_slice_in_dim(
@@ -326,7 +331,7 @@
     )
     full_up = lax.all_gather(up_mine, "fsdp", axis=0, tiled=True)
     down_mine = take(down_late, blk * hidden_rows, hidden_rows)
-    full_down = jnp.concatenate(in_order(doubled(down_mine, "fsdp"), own))
+    full_down = lax.all_gather(down_mine, "fsdp", axis=0, tiled=True)
     up_shift = jnp.concatenate(
         [
             lax.dynamic_slice_in_dim(up_bias, (i * blocks + blk) * hidden_rows, hidden_rows)
@@ -342,21 +347,21 @@
     )
     own_count = counts[0, blk * seqs + seq]
     own_valid = lax.broadcasted_iota(jnp.int32, (rows, 1), 0) < own_count
-    key_counts = jnp.stack(
-        [counts[0, (blk ^ m) * seqs + (seq ^ k)] for m in range(blocks) for k in range(seqs)]
-    )
+    place = jnp.stack([blk, seq]).astype(jnp.int32)
     grad_rows = jnp.where(own_valid, grad_late[0], 0.0)
     d_outcome = grad_rows.astype(BF)
     d_outcome_all = jnp.concatenate(from_all(d_outcome, "blk"))
 
     key_value = (
-        dot_nn(normed1_all, qkv_full[:, head_width:]) + qkv_shift[head_width:]
+        dot_nn(after(normed1_all, d_outcome_all), qkv_full[:, head_width:])
+        + qkv_shift[head_width:]
     ).astype(BF)
     kv_blocks = from_all(key_value, "blk")
     queries = (
         dot_nn(after(normed1_all, key_value), qkv_full[:, :head_width]) + qkv_shift[:head_width]
     ).astype(BF)
-    attended, log_total = attend(key_counts, queries, kv_blocks, rows)
+    queries = after(queries, full_out)
+    attended, log_total = attend(place, counts, queries, kv_blocks, rows)
     att_pieces = [attended[:rows]] + [
         swap(attended[k * rows : (k + 1) * rows], "seq", k) for k in range(1, seqs)
     ]
@@ -390,30 +395,14 @@
     d_attended = jnp.concatenate(
         [d_head_pieces[0]] + [swap(d_head_pieces[k], "seq", k) for k in range(1, seqs)]
     )
-    branch_late, att_late, d_up_late = after((d_branch, token_att, d_up), *d_head_pieces)
-    att_all = jnp.concatenate(from_all(att_late, "blk"))
-    branch_all = jnp.concatenate(
-        [
-            lax.dynamic_slice_in_dim(branch_late, blk * out_width, out_width, axis=1),
-        ]
-        + [
-            swap(
-                lax.dynamic_slice_in_dim(branch_late, (blk ^ m) * out_width, out_width, axis=1),
-                "blk",
-                m,
-            )
-            for m in range(1, blocks)
-        ]
-    )
+    d_attended = after(d_attended, half_down)
+    back = attend_back(place, counts, queries, log_total, d_attended, kv_blocks, rows)
+    own_down = owner_sums(half_down, own)
+    att_late, d_up_late = after((token_att, d_up), back)
     grads_up = jnp.concatenate(
-        [dot_tn(normed2_all, d_up_late).astype(BF), dot_tn(att_all, branch_all).astype(BF)], axis=1
-    )
-    half_up = core_sums(grads_up.reshape(owners, own_rows, hidden_width + out_width), own)
-
-    d_attended = after(d_attended, half_down, half_up)
-    back = attend_back(key_counts, queries, log_total, d_attended, kv_blocks, rows)
-    own_down = owner_sums(half_down, own)
-    own_up = owner_sums(half_up, own)
+        [dot_tn(normed2_all, d_up_late).astype(BF), dot_tn(att_late, d_branch).astype(BF)], axis=1
+    )
+    half_up = core_sums(grads_up.reshape(owners, own_rows, hidden_width + width), own)
     d_query, d_kv = back[0], back[1]
     for m in range(1, blocks):
         d_kv = d_kv + swap(back[1 + m], "blk", m).astype(F32)
@@ -421,17 +410,25 @@
     d_projected = jnp.concatenate([d_query, d_kv], axis=1)
     d_normed1_parts = dot_nt(d_projected, qkv_full).astype(BF)
     d_normed1 = split_sums(d_normed1_parts, "seq")
+
+    normed1_late = after(normed1_all, d_normed1_parts)
     sum_down = chunk_sums(own_down, "seq", seq)
-
-    normed1_late, hidden_late = after((normed1_all, hidden), d_normed1_parts)
     half_qkv = core_sums(
         dot_tn(normed1_late, d_projected).astype(BF).reshape(owners, own_rows, 3 * head_width), own
     )
+    own_up = owner_sums(half_up, own)
+    own_out = own_up[:, hidden_width:]
+    kept_out = lax.dynamic_slice_in_dim(own_out, blk * out_width, out_width, axis=1)
+    for m in range(1, blocks):
+        sent = lax.dynamic_slice_in_dim(own_out, (blk ^ m) * out_width, out_width, axis=1)
+        kept_out = kept_out + swap(sent.astype(BF), "blk", m).astype(F32)
+    sum_up = chunk_sums(
+        jnp.concatenate([own_up[:, :hidden_width], kept_out], axis=1), "seq", seq
+    )
+    d_normed1, hidden_late = after((d_normed1, hidden), kept_out)
     outcome = split_sums(dot_nn(hidden_late, full_down), "blk")
     activations = jnp.where(own_valid, middle + outcome + biases[3], 0.0)
-    sum_up = chunk_sums(own_up, "seq", seq)
     sum_qkv = chunk_sums(owner_sums(half_qkv, own), "blk", blk)
-    d_normed1 = after(d_normed1, sum_down)
     d_inputs, d_gain_one, d_shift_one = norm_back(d_normed1, unit1, inverse1, gains[0])
     grad_tokens = d_middle + d_inputs
 
@@ -452,7 +449,7 @@
             jnp.where(is_blk, up_sums, 0.0).reshape(-1),
         ]
     ).reshape(-1, 128)
-    vectors = sum_over(vectors, ("fsdp", "seq", "blk")).reshape(-1)
+    vectors = sum_over(after(vectors, sum_up), ("fsdp", "seq", "blk")).reshape(-1)
     mine = lax.dynamic_slice_in_dim(
         vectors[: 8 * width].reshape(8, width), own * own_rows, own_rows, axis=1
     )
@@ -461,23 +458,20 @@
     )
 
     def spread(array):
-        over_seq = from_all(array, "seq")
-        over_blk = from_all(jnp.stack(over_seq), "blk")
-        return [[piece[k] for k in range(seqs)] for piece in over_blk]
+        over_seq = [from_all(one, "blk") for one in from_all(array, "seq")]
+        return [[one[m] for one in over_seq] for m in range(blocks)]
 
     chunk, seq_rows, blk_rows = hidden_rows // seqs, own_rows // seqs, own_rows // blocks
     (grad_down,) = put_in_place(
         spread(sum_down),
-        blk,
-        seq,
+        place,
         [(blocks * hidden_rows, width)],
         [lambda b, k: [(0, width, b * hidden_rows + k * chunk, 0)]],
         "place_down",
     )
     grad_up, grad_w_out = put_in_place(
         spread(sum_up),
-        blk,
-        seq,
+        place,
         [(own_rows, blocks * hidden_width), (own_rows, width)],
         [
             lambda b, k: [
@@ -489,9 +483,8 @@
         "place_up",
     )
     (grad_qkv,) = put_in_place(
-        spread(sum_qkv),
-        blk,
-        seq,
+        spread(after(sum_qkv, sum_up)),
+        place,
         [(own_rows, 3 * width)],
         [
             lambda b, k: [

time: 270 us -> 295 us (1.093); the launches traced: 266 us -> 295 us
  starting transfers between devices: 61.9 us -> 84.6 us
  matrix products: 16.5 us -> 21.3 us
    ppermute x56 -> x64, starting transfers between devices: 61.8 us -> 84.5 us  [swap(): lax.ppermute(array, axis, [(i, i ^ bits) for i in range(lax.axis_size(axi...]
    dot_general x7, matrix products: 4.62 us -> 12.1 us  [dot_nt(): lax.dot_general(left_side, right_side, (((1,), (1,)), ((), ())), preferre...]
    another operation x1 -> x0, local copies, waits for them, and re-layouts: 5.25 us -> none  [shards(): jnp.stack([counts[0, (blk ^ m) * seqs + (seq ^ k)] for m in range(blocks)...]
    unnamed x120 -> x142, local copies, waits for them, and re-layouts: 2.89 us -> 6.92 us
    ppermute x56 -> x64, waiting for transfers between devices: 96.3 us -> 96.8 us  [swap(): lax.ppermute(array, axis, [(i, i ^ bits) for i in range(lax.axis_size(axi...]
  transfers between devices with their start and end apart: 58 -> 66, of which waited for: 29 -> 29; matrix products, arithmetic and copies ran while one was open for 24% -> 18% of each run, Pallas kernels for 6% -> 4%
where the time goes in v1:
time: 295 us
  waiting for transfers between devices  96.9 us (33%)
  starting transfers between devices  84.6 us (29%)
  other arithmetic  30.5 us (10%)
  local copies, waits for them, and re-layouts  24.9 us (8%)
  matrix products  21.3 us (7%)
  Pallas kernels  20.8 us (7%)
  between operations  15.4 us (5%)
    ppermute x64, waiting for transfers between devices, swap(): lax.ppermute(array, axis, [(i, i ^ bits) for i in range(lax.axis_size(axi...  96.8 us
    ppermute x64, starting transfers between devices, swap(): lax.ppermute(array, axis, [(i, i ^ bits) for i in range(lax.axis_size(axi...  84.5 us
    dot_general x7, matrix products, dot_nt(): lax.dot_general(left_side, right_side, (((1,), (1,)), ((), ())), preferre...  12.1 us
    pallas_call x3, Pallas kernels, put_in_place(): pl.pallas_call(functools.partial(place_kernel, seqs, blocks, layouts), ou...  11.3 us
    unnamed x142, local copies, waits for them, and re-layouts  6.92 us
    dot_general x5, matrix products, dot_nn(): lax.dot_general(left_side, right_side, (((1,), (0,)), ((), ())), preferre...  6.23 us
  transfers between devices with their start and end apart: 66, of which 29 were waited for; matrix products, arithmetic and copies ran while one was open for 18% of the time, Pallas kernels for 4%

profile of v1, /device:TPU:0, one launch (start us, length us, event | category | flops | bytes accessed | tf_op | source)
XLA Modules:
  0.0 294.6 jit_solution(2158936072036333845)
XLA Ops:
  15.9 5.1 %collective-permute-start.2 = (bf16[128,768]{1,0:T(8,128)(2,1)S(1)}, bf16[128,768]{1,0:T(8,128)(2,1)S(1)}, u32[]{:S(2)}, u32[]{:S(2)}) collective-permute-start(bf16[128,768]{1,0:T(8,128)(2,1)S(1)} %add_convert_fusion.2), channel_id=1, source_target_pairs={{0,3},{1,2},{2,1},{3,0},{4,7},{5,6},{6,5},{7,4},{8,11},{9,10},{10,... | collective-permute-start | bytes 589832 | tf_op jit(solution)/shard_map/ppermute | solution.py:38
  32.2 5.5 %collective-permute-done.1 = bf16[128,768]{1,0:T(8,128)(2,1)} collective-permute-done((bf16[128,768]{1,0:T(8,128)(2,1)S(1)}, bf16[128,768]{1,0:T(8,128)(2,1)}, u32[]{:S(2)}, u32[]{:S(2)}) %collective-permute-start.1) | collective-permute-done | bytes 196640 | tf_op jit(solution)/shard_map/ppermute | solution.py:38
  38.9 5.5 %collective-permute-done.7 = bf16[192,768]{1,0:T(8,128)(2,1)} collective-permute-done((bf16[192,768]{1,0:T(8,128)(2,1)}, bf16[192,768]{1,0:T(8,128)(2,1)}, u32[]{:S(2)}, u32[]{:S(2)}) %collective-permute-start.7) | collective-permute-done | bytes 294944 | tf_op jit(solution)/shard_map/ppermute | solution.py:38
  48.9 8.3 %collective-permute-done.10.refs_1_ = bf16[512,384]{1,0:T(8,128)(2,1)S(1)} collective-permute-done((bf16[512,384]{1,0:T(8,128)(2,1)S(1)}, bf16[512,384]{1,0:T(8,128)(2,1)S(1)}, u32[]{:S(2)}, u32[]{:S(2)}) %collective-permute-start.10) | collective-permute-done | bytes 393248 | tf_op jit(solution)/shard_map/ppermute | solution.py:38
  57.1 3.9 %attend.1 = (bf16[512,192]{1,0:T(8,128)(2,1)S(1)}, f32[3,512]{1,0:T(4,128)S(1)}) custom-call(s32[2]{0:T(128)S(1)} %pad_add_fusion.place_ref, s32[1,8]{1,0:T(1,128)S(1)} %copy-done.2, bf16[512,192]{1,0:T(8,128)(2,1)S(1)} %fusion.7.q_ref, bf16[512,384]{1,0:T(8,128)(2,1)S(1)} %fusion.6.refs_0_, bf16[512,384]{1,0:T(8,128)(2,1)S(1)} %collective-permute-done.10.refs_1_), custom_call_target="tpu_custom_call" | custom-call | flops 402653184 | bytes 1179648 | tf_op jit(solution)/shard_map/attend/pallas_call | solution.py:117
  61.7 3.5 %collective-permute-start.11 = (bf16[128,192]{1,0:T(8,128)(2,1)}, bf16[128,192]{1,0:T(8,128)(2,1)S(1)}, u32[]{:S(2)}, u32[]{:S(2)}) collective-permute-start(bf16[128,192]{1,0:T(8,128)(2,1)} %get-tuple-element.110), channel_id=1, source_target_pairs={{0,3},{1,2},{2,1},{3,0},{4,7},{5,6},{6,5},{7,4},{8,11},{9,10},{10,... | collective-permute-start | bytes 147464 | tf_op jit(solution)/shard_map/ppermute | solution.py:38
  65.2 3.0 %collective-permute-start.13 = (bf16[128,192]{1,0:T(8,128)(2,1)}, bf16[128,192]{1,0:T(8,128)(2,1)S(1)}, u32[]{:S(2)}, u32[]{:S(2)}) collective-permute-start(bf16[128,192]{1,0:T(8,128)(2,1)} %get-tuple-element.111), channel_id=1, source_target_pairs={{0,1},{1,0},{2,3},{3,2},{4,5},{5,4},{6,7},{7,6},{8,9},{9,8},{10,11... | collective-permute-start | bytes 147464 | tf_op jit(solution)/shard_map/ppermute | solution.py:38
  71.3 2.5 collective-permute-done.12
  78.5 3.7 %collective-permute-done.14 = bf16[128,768]{1,0:T(8,128)(2,1)S(1)} collective-permute-done((bf16[128,768]{1,0:T(8,128)(2,1)S(1)}, bf16[128,768]{1,0:T(8,128)(2,1)S(1)}, u32[]{:S(2)}, u32[]{:S(2)}) %collective-permute-start.14) | collective-permute-done | bytes 196640 | tf_op jit(solution)/shard_map/ppermute | solution.py:38
  86.1 4.0 %convert_reduce_fusion = (f32[1536]{0:T(1024)S(1)}, bf16[256,1536]{1,0:T(8,128)(2,1)S(1)}, bf16[256,1536]{1,0:T(8,128)(2,1)}) fusion(f32[256,1536]{1,0:T(8,128)S(1)} %fusion.65, f32[1536]{0:T(1024)S(1)} %maximum_convert_fusion, bf16[256,768]{1,0:T(8,128)(2,1)} %pad_maximum_fusion.7, bf16[768,1536]{1,0:T(8,128)(2,1)} %all-gather.5.cloned.1.call-done), kind=kOutput, calls=%fused_computation.24 | convolution fusion | flops 609876480 | bytes 5910528 | tf_op jit(solution)/shard_map/dot_general | solution.py:20
  90.2 2.8 convolution_convert_fusion.5
  101.5 2.5 convert_reduce_fusion.3
  110.7 2.7 collective-permute-start.17
  116.5 3.2 %collective-permute-done.18 = bf16[128,192]{1,0:T(8,128)(2,1)} collective-permute-done((bf16[128,192]{1,0:T(8,128)(2,1)}, bf16[128,192]{1,0:T(8,128)(2,1)}, u32[]{:S(2)}, u32[]{:S(2)}) %collective-permute-start.18) | collective-permute-done | bytes 49184 | tf_op jit(solution)/shard_map/ppermute | solution.py:38
  122.3 5.7 %attend_back.1 = (bf16[512,192]{1,0:T(8,128)(2,1)S(1)}, f32[512,384]{1,0:T(8,128)S(1)}, bf16[512,384]{1,0:T(8,128)(2,1)S(1)}) custom-call(s32[2]{0:T(128)S(1)} %pad_add_fusion.place_ref, s32[1,8]{1,0:T(1,128)S(1)} %copy-done.2, bf16[512,192]{1,0:T(8,128)(2,1)S(1)} %fusion.7.q_ref, f32[3,512]{1,0:T(4,128)S(1)} %get-tuple-element.41.log_ref, ...), custom_call_target="tpu_custom_call" | custom-call | flops 1006632960 | bytes 2555904 | tf_op jit(solution)/shard_map/attend_back/pallas_call | solution.py:140
  157.7 4.8 %collective-permute-done.55 = bf16[96,768]{1,0:T(8,128)(2,1)} collective-permute-done((bf16[96,768]{1,0:T(8,128)(2,1)}, bf16[96,768]{1,0:T(8,128)(2,1)}, u32[]{:S(2)}, u32[]{:S(2)}) %collective-permute-start.55) | collective-permute-done | bytes 147488 | tf_op jit(solution)/shard_map/ppermute | solution.py:38
  163.8 5.7 %collective-permute-done.21 = bf16[128,768]{1,0:T(8,128)(2,1)S(1)} collective-permute-done((bf16[128,768]{1,0:T(8,128)(2,1)}, bf16[128,768]{1,0:T(8,128)(2,1)S(1)}, u32[]{:S(2)}, u32[]{:S(2)}) %collective-permute-start.21) | collective-permute-done | bytes 196640 | tf_op jit(solution)/shard_map/ppermute | solution.py:38
  171.2 9.7 %collective-permute-start.58 = (bf16[96,768]{1,0:T(8,128)(2,1)S(1)}, bf16[96,768]{1,0:T(8,128)(2,1)S(1)}, u32[]{:S(2)}, u32[]{:S(2)}) collective-permute-start(bf16[96,768]{1,0:T(8,128)(2,1)S(1)} %fusion.39.refs_0_), channel_id=1, source_target_pairs={{0,2},{1,3},{2,0},{3,1},{4,6},{5,7},{6,4},{7,5},{8,10},{9,11},{10,... | collective-permute-start | bytes 442376 | tf_op jit(solution)/shard_map/ppermute | solution.py:38
  180.8 3.8 %collective-permute-done.22 = bf16[128,768]{1,0:T(8,128)(2,1)S(1)} collective-permute-done((bf16[128,768]{1,0:T(8,128)(2,1)S(1)}, bf16[128,768]{1,0:T(8,128)(2,1)S(1)}, u32[]{:S(2)}, u32[]{:S(2)}) %collective-permute-start.22) | collective-permute-done | bytes 196640 | tf_op jit(solution)/shard_map/ppermute | solution.py:38
  187.8 3.0 %collective-permute-done.58.refs_2_ = bf16[96,768]{1,0:T(8,128)(2,1)S(1)} collective-permute-done((bf16[96,768]{1,0:T(8,128)(2,1)S(1)}, bf16[96,768]{1,0:T(8,128)(2,1)S(1)}, u32[]{:S(2)}, u32[]{:S(2)}) %collective-permute-start.58) | collective-permute-done | bytes 147488 | tf_op jit(solution)/shard_map/ppermute | solution.py:38
  193.6 3.7 %collective-permute-done.62.refs_6_ = bf16[96,768]{1,0:T(8,128)(2,1)S(1)} collective-permute-done((bf16[96,768]{1,0:T(8,128)(2,1)S(1)}, bf16[96,768]{1,0:T(8,128)(2,1)S(1)}, u32[]{:S(2)}, u32[]{:S(2)}) %collective-permute-start.62) | collective-permute-done | bytes 147488 | tf_op jit(solution)/shard_map/ppermute | solution.py:38
  198.8 3.7 %place_down.1 = f32[768,768]{1,0:T(8,128)} custom-call(s32[2]{0:T(128)S(1)} %pad_add_fusion.place_ref, bf16[96,768]{1,0:T(8,128)(2,1)S(1)} %fusion.39.refs_0_, bf16[96,768]{1,0:T(8,128)(2,1)S(1)} %collective-permute-done.57.refs_1_, bf16[96,768]{1,0:T(8,128)(2,1)S(1)} %collective-permute-done.58.refs_2_, ...), custom_call_target="tpu_custom_call" | custom-call | bytes 3538944 | tf_op jit(solution)/shard_map/place_down/pallas_call | solution.py:272
  205.2 2.9 collective-permute-done.26
  213.2 4.7 %collective-permute-done.28 = bf16[48,1920]{1,0:T(8,128)(2,1)S(1)} collective-permute-done((bf16[48,1920]{1,0:T(8,128)(2,1)S(1)}, bf16[48,1920]{1,0:T(8,128)(2,1)S(1)}, u32[]{:S(2)}, u32[]{:S(2)}) %collective-permute-start.28) | collective-permute-done | bytes 184352 | tf_op jit(solution)/shard_map/ppermute | solution.py:38
  217.9 4.4 %collective-permute-done.29 = bf16[48,1920]{1,0:T(8,128)(2,1)S(1)} collective-permute-done((bf16[48,1920]{1,0:T(8,128)(2,1)S(1)}, bf16[48,1920]{1,0:T(8,128)(2,1)S(1)}, u32[]{:S(2)}, u32[]{:S(2)}) %collective-permute-start.29) | collective-permute-done | bytes 184352 | tf_op jit(solution)/shard_map/ppermute | solution.py:38
  227.7 3.3 %collective-permute-start.33 = (f32[72,128]{1,0:T(8,128)S(1)}, f32[72,128]{1,0:T(8,128)S(1)}, u32[]{:S(2)}, u32[]{:S(2)}) collective-permute-start(f32[72,128]{1,0:T(8,128)S(1)} %add.389), channel_id=1, source_target_pairs={{0,1},{1,0},{2,3},{3,2},{4,5},{5,4},{6,7},{7,6},{8,9},{9,8},{10,11... | collective-permute-start | bytes 110600 | tf_op jit(solution)/shard_map/ppermute | solution.py:38
  245.9 4.9 %collective-permute-start.47 = (bf16[48,1920]{1,0:T(8,128)(2,1)S(1)}, bf16[48,1920]{1,0:T(8,128)(2,1)S(1)}, u32[]{:S(2)}, u32[]{:S(2)}) collective-permute-start(bf16[48,1920]{1,0:T(8,128)(2,1)S(1)} %fusion.29.refs_0_), channel_id=1, source_target_pairs={{0,2},{1,3},{2,0},{3,1},{4,6},{5,7},{6,4},{7,5},{8,10},{9,11},{10,... | collective-permute-start | bytes 552968 | tf_op jit(solution)/shard_map/ppermute | solution.py:38
  250.9 5.9 %collective-permute-done.40.refs_2_ = bf16[96,576]{1,0:T(8,128)(2,1)S(1)} collective-permute-done((bf16[96,576]{1,0:T(8,128)(2,1)S(1)}, bf16[96,576]{1,0:T(8,128)(2,1)S(1)}, u32[]{:S(2)}, u32[]{:S(2)}) %collective-permute-start.40) | collective-permute-done | bytes 110624 | tf_op jit(solution)/shard_map/ppermute | solution.py:38
  260.6 3.7 %collective-permute-done.47.refs_2_ = bf16[48,1920]{1,0:T(8,128)(2,1)S(1)} collective-permute-done((bf16[48,1920]{1,0:T(8,128)(2,1)S(1)}, bf16[48,1920]{1,0:T(8,128)(2,1)S(1)}, u32[]{:S(2)}, u32[]{:S(2)}) %collective-permute-start.47) | collective-permute-done | bytes 184352 | tf_op jit(solution)/shard_map/ppermute | solution.py:38
  270.4 9.7 %collective-permute-done.43.refs_5_ = bf16[96,576]{1,0:T(8,128)(2,1)S(1)} collective-permute-done((bf16[96,576]{1,0:T(8,128)(2,1)S(1)}, bf16[96,576]{1,0:T(8,128)(2,1)S(1)}, u32[]{:S(2)}, u32[]{:S(2)}) %collective-permute-start.43) | collective-permute-done | bytes 110624 | tf_op jit(solution)/shard_map/ppermute | solution.py:38
  280.1 3.3 %place_qkv.1 = f32[192,2304]{1,0:T(8,128)} custom-call(s32[2]{0:T(128)S(1)} %pad_add_fusion.place_ref, bf16[96,576]{1,0:T(8,128)(2,1)S(1)} %fusion.44.refs_0_, bf16[96,576]{1,0:T(8,128)(2,1)S(1)} %collective-permute-done.39.refs_1_, bf16[96,576]{1,0:T(8,128)(2,1)S(1)} %collective-permute-done.40.refs_2_, ...), custom_call_target="tpu_custom_call" | custom-call | bytes 2654208 | tf_op jit(solution)/shard_map/place_qkv/pallas_call | solution.py:272
  283.4 4.3 %place_up.1 = (f32[192,3072]{1,0:T(8,128)}, f32[192,768]{1,0:T(8,128)}) custom-call(s32[2]{0:T(128)S(1)} %pad_add_fusion.place_ref, bf16[48,1920]{1,0:T(8,128)(2,1)S(1)} %fusion.29.refs_0_, bf16[48,1920]{1,0:T(8,128)(2,1)S(1)} %collective-permute-done.46.refs_1_, bf16[48,1920]{1,0:T(8,128)(2,1)S(1)} %collective-permute-done.47.refs_2_, ...), custom_call_target="tpu_custom_call" | custom-call | bytes 4423680 | tf_op jit(solution)/shard_map/place_up/pallas_call | solution.py:272
  (370 shorter events, 136.0 us)
Async XLA Ops:
  7.2 76.5 %all-gather.3.cloned.1.call-start = ((), (), s32[]{:S(2)}) async-start(), calls=%async_computation | async-start | bytes 2949120 | tf_op jit(solution)/shard_map/all_gather | solution.py:334
  15.8 70.3 %all-gather.5.cloned.1.call-start = ((), (), s32[]{:S(2)}) async-start(), calls=%async_computation.1 | async-start | bytes 2949120 | tf_op jit(solution)/shard_map/all_gather | solution.py:332
  15.9 12.9 %collective-permute-start.2 = (bf16[128,768]{1,0:T(8,128)(2,1)S(1)}, bf16[128,768]{1,0:T(8,128)(2,1)S(1)}, u32[]{:S(2)}, u32[]{:S(2)}) collective-permute-start(bf16[128,768]{1,0:T(8,128)(2,1)S(1)} %add_convert_fusion.2), channel_id=1, source_target_pairs={{0,3},{1,2},{2,1},{3,0},{4,7},{5,6},{6,5},{7,4},{8,11},{9,10},{10,... | collective-permute-start | bytes 589832 | tf_op jit(solution)/shard_map/ppermute | solution.py:38
  20.9 16.8 %collective-permute-start.1 = (bf16[128,768]{1,0:T(8,128)(2,1)S(1)}, bf16[128,768]{1,0:T(8,128)(2,1)}, u32[]{:S(2)}, u32[]{:S(2)}) collective-permute-start(bf16[128,768]{1,0:T(8,128)(2,1)S(1)} %add_convert_fusion.2), channel_id=1, source_target_pairs={{0,2},{1,3},{2,0},{3,1},{4,6},{5,7},{6,4},{7,5},{8,10},{9,11},{10,... | collective-permute-start | bytes 589832 | tf_op jit(solution)/shard_map/ppermute | solution.py:38
  20.9 16.8 %collective-permute-start = (bf16[128,768]{1,0:T(8,128)(2,1)S(1)}, bf16[128,768]{1,0:T(8,128)(2,1)}, u32[]{:S(2)}, u32[]{:S(2)}) collective-permute-start(bf16[128,768]{1,0:T(8,128)(2,1)S(1)} %add_convert_fusion.2), channel_id=1, source_target_pairs={{0,1},{1,0},{2,3},{3,2},{4,5},{5,4},{6,7},{7,6},{8,9},{9,8},{10,11... | collective-permute-start | bytes 589832 | tf_op jit(solution)/shard_map/ppermute | solution.py:38
  28.7 15.6 %collective-permute-start.7 = (bf16[192,768]{1,0:T(8,128)(2,1)}, bf16[192,768]{1,0:T(8,128)(2,1)}, u32[]{:S(2)}, u32[]{:S(2)}) collective-permute-start(bf16[192,768]{1,0:T(8,128)(2,1)} %param.18), channel_id=1, source_target_pairs={{0,16},{8,24},{16,0},{24,8},{1,17},{9,25},{17,1},{25,9},{2,18},{10... | collective-permute-start | bytes 884744 | tf_op jit(solution)/shard_map/ppermute | solution.py:38
  31.0 13.4 %collective-permute-start.6 = (bf16[192,576]{1,0:T(8,128)(2,1)S(1)}, bf16[192,576]{1,0:T(8,128)(2,1)S(1)}, u32[]{:S(2)}, u32[]{:S(2)}) collective-permute-start(bf16[192,576]{1,0:T(8,128)(2,1)S(1)} %copy-done.48), channel_id=1, source_target_pairs={{0,8},{8,0},{16,24},{24,16},{1,9},{9,1},{17,25},{25,17},{2,10},{10... | collective-permute-start | bytes 663560 | tf_op jit(solution)/shard_map/ppermute | solution.py:38
  32.2 12.2 %collective-permute-start.5 = (bf16[192,576]{1,0:T(8,128)(2,1)S(1)}, bf16[192,576]{1,0:T(8,128)(2,1)S(1)}, u32[]{:S(2)}, u32[]{:S(2)}) collective-permute-start(bf16[192,576]{1,0:T(8,128)(2,1)S(1)} %collective-permute-done.4), channel_id=1, source_target_pairs={{0,8},{8,0},{16,24},{24,16},{1,9},{9,1},{17,25},{25,17},{2,10},{10... | collective-permute-start | bytes 663560 | tf_op jit(solution)/shard_map/ppermute | solution.py:38
  45.6 11.6 %collective-permute-start.10 = (bf16[512,384]{1,0:T(8,128)(2,1)S(1)}, bf16[512,384]{1,0:T(8,128)(2,1)S(1)}, u32[]{:S(2)}, u32[]{:S(2)}) collective-permute-start(bf16[512,384]{1,0:T(8,128)(2,1)S(1)} %fusion.6.refs_0_), channel_id=1, source_target_pairs={{0,4},{4,0},{1,5},{5,1},{2,6},{6,2},{3,7},{7,3},{8,12},{12,8},{9,1... | collective-permute-start | bytes 1179656 | tf_op jit(solution)/shard_map/ppermute | solution.py:38
  97.8 22.9 %collective-permute-start.19 = (bf16[2,384,768]{2,1,0:T(8,128)(2,1)}, bf16[2,384,768]{2,1,0:T(8,128)(2,1)}, u32[]{:S(2)}, u32[]{:S(2)}) collective-permute-start(bf16[2,384,768]{2,1,0:T(8,128)(2,1)} %dynamic-slice_bitcast_fusion.1), channel_id=1, source_target_pairs={{0,8},{8,0},{16,24},{24,16},{1,9},{9,1},{17,25},{25,17},{2,10},{10... | collective-permute-start | bytes 3538952 | tf_op jit(solution)/shard_map/ppermute | solution.py:38
  130.4 12.4 %collective-permute-start.53 = (bf16[1,384,768]{2,1,0:T(8,128)(2,1)}, bf16[1,384,768]{2,1,0:T(8,128)(2,1)}, u32[]{:S(2)}, u32[]{:S(2)}) collective-permute-start(bf16[1,384,768]{2,1,0:T(8,128)(2,1)} %dynamic-slice_convert_fusion.1), channel_id=1, source_target_pairs={{0,16},{8,24},{16,0},{24,8},{1,17},{9,25},{17,1},{25,9},{2,18},{10... | collective-permute-start | bytes 1769480 | tf_op jit(solution)/shard_map/ppermute | solution.py:38
  136.7 12.2 %collective-permute-start.24 = (bf16[2,192,2304]{2,1,0:T(8,128)(2,1)}, bf16[2,192,2304]{2,1,0:T(8,128)(2,1)}, u32[]{:S(2)}, u32[]{:S(2)}) collective-permute-start(bf16[2,192,2304]{2,1,0:T(8,128)(2,1)} %dynamic-slice_bitcast_fusion), channel_id=1, source_target_pairs={{0,8},{8,0},{16,24},{24,16},{1,9},{9,1},{17,25},{25,17},{2,10},{10... | collective-permute-start | bytes 5308424 | tf_op jit(solution)/shard_map/ppermute | solution.py:38
  146.6 15.9 %collective-permute-start.55 = (bf16[96,768]{1,0:T(8,128)(2,1)}, bf16[96,768]{1,0:T(8,128)(2,1)}, u32[]{:S(2)}, u32[]{:S(2)}) collective-permute-start(bf16[96,768]{1,0:T(8,128)(2,1)} %get-tuple-element.87), channel_id=1, source_target_pairs={{0,2},{1,3},{2,0},{3,1},{4,6},{5,7},{6,4},{7,5},{8,10},{9,11},{10,... | collective-permute-start | bytes 442376 | tf_op jit(solution)/shard_map/ppermute | solution.py:38
  153.7 48.9 %collective-permute-start.25 = (bf16[1,192,2304]{2,1,0:T(8,128)(2,1)}, bf16[1,192,2304]{2,1,0:T(8,128)(2,1)S(1)}, u32[]{:S(2)}, u32[]{:S(2)}) collective-permute-start(bf16[1,192,2304]{2,1,0:T(8,128)(2,1)} %dynamic-slice_convert_fusion), channel_id=1, source_target_pairs={{0,16},{8,24},{16,0},{24,8},{1,17},{9,25},{17,1},{25,9},{2,18},{10... | collective-permute-start | bytes 2654216 | tf_op jit(solution)/shard_map/ppermute | solution.py:38
  155.7 30.0 %collective-permute-start.36 = (bf16[2,192,576]{2,1,0:T(8,128)(2,1)S(1)}, bf16[2,192,576]{2,1,0:T(8,128)(2,1)S(1)}, u32[]{:S(2)}, u32[]{:S(2)}) collective-permute-start(bf16[2,192,576]{2,1,0:T(8,128)(2,1)S(1)} %dynamic-slice_bitcast_fusion.2), channel_id=1, source_target_pairs={{0,8},{8,0},{16,24},{24,16},{1,9},{9,1},{17,25},{25,17},{2,10},{10... | collective-permute-start | bytes 1327112 | tf_op jit(solution)/shard_map/ppermute | solution.py:38
  155.8 13.7 %collective-permute-start.21 = (bf16[128,768]{1,0:T(8,128)(2,1)}, bf16[128,768]{1,0:T(8,128)(2,1)S(1)}, u32[]{:S(2)}, u32[]{:S(2)}) collective-permute-start(bf16[128,768]{1,0:T(8,128)(2,1)} %get-tuple-element.103), channel_id=1, source_target_pairs={{0,1},{1,0},{2,3},{3,2},{4,5},{5,4},{6,7},{7,6},{8,9},{9,8},{10,11... | collective-permute-start | bytes 589832 | tf_op jit(solution)/shard_map/ppermute | solution.py:38
  156.7 14.5 %collective-permute-start.23 = (bf16[128,768]{1,0:T(8,128)(2,1)S(1)}, bf16[128,768]{1,0:T(8,128)(2,1)S(1)}, u32[]{:S(2)}, u32[]{:S(2)}) collective-permute-start(bf16[128,768]{1,0:T(8,128)(2,1)S(1)} %get-tuple-element.104), channel_id=1, source_target_pairs={{0,3},{1,2},{2,1},{3,0},{4,7},{5,6},{6,5},{7,4},{8,11},{9,10},{10,... | collective-permute-start | bytes 589832 | tf_op jit(solution)/shard_map/ppermute | solution.py:38
  162.5 22.2 %collective-permute-start.22 = (bf16[128,768]{1,0:T(8,128)(2,1)S(1)}, bf16[128,768]{1,0:T(8,128)(2,1)S(1)}, u32[]{:S(2)}, u32[]{:S(2)}) collective-permute-start(bf16[128,768]{1,0:T(8,128)(2,1)S(1)} %get-tuple-element.105), channel_id=1, source_target_pairs={{0,2},{1,3},{2,0},{3,1},{4,6},{5,7},{6,4},{7,5},{8,10},{9,11},{10,... | collective-permute-start | bytes 589832 | tf_op jit(solution)/shard_map/ppermute | solution.py:38
  169.5 17.0 %collective-permute-start.59 = (bf16[96,768]{1,0:T(8,128)(2,1)S(1)}, bf16[96,768]{1,0:T(8,128)(2,1)S(1)}, u32[]{:S(2)}, u32[]{:S(2)}) collective-permute-start(bf16[96,768]{1,0:T(8,128)(2,1)S(1)} %fusion.39.refs_0_), channel_id=1, source_target_pairs={{0,3},{1,2},{2,1},{3,0},{4,7},{5,6},{6,5},{7,4},{8,11},{9,10},{10,... | collective-permute-start | bytes 442376 | tf_op jit(solution)/shard_map/ppermute | solution.py:38
  171.2 19.7 %collective-permute-start.58 = (bf16[96,768]{1,0:T(8,128)(2,1)S(1)}, bf16[96,768]{1,0:T(8,128)(2,1)S(1)}, u32[]{:S(2)}, u32[]{:S(2)}) collective-permute-start(bf16[96,768]{1,0:T(8,128)(2,1)S(1)} %fusion.39.refs_0_), channel_id=1, source_target_pairs={{0,2},{1,3},{2,0},{3,1},{4,6},{5,7},{6,4},{7,5},{8,10},{9,11},{10,... | collective-permute-start | bytes 442376 | tf_op jit(solution)/shard_map/ppermute | solution.py:38
  203.7 18.8 %collective-permute-start.38 = (bf16[96,576]{1,0:T(8,128)(2,1)S(1)}, bf16[96,576]{1,0:T(8,128)(2,1)S(1)}, u32[]{:S(2)}, u32[]{:S(2)}) collective-permute-start(bf16[96,576]{1,0:T(8,128)(2,1)S(1)} %fusion.48), channel_id=1, source_target_pairs={{0,4},{4,0},{1,5},{5,1},{2,6},{6,2},{3,7},{7,3},{8,12},{12,8},{9,1... | collective-permute-start | bytes 331784 | tf_op jit(solution)/shard_map/ppermute | solution.py:38
  209.1 13.2 %collective-permute-start.29 = (bf16[48,1920]{1,0:T(8,128)(2,1)S(1)}, bf16[48,1920]{1,0:T(8,128)(2,1)S(1)}, u32[]{:S(2)}, u32[]{:S(2)}) collective-permute-start(bf16[48,1920]{1,0:T(8,128)(2,1)S(1)} %get-tuple-element.83), channel_id=1, source_target_pairs={{0,2},{1,3},{2,0},{3,1},{4,6},{5,7},{6,4},{7,5},{8,10},{9,11},{10,... | collective-permute-start | bytes 552968 | tf_op jit(solution)/shard_map/ppermute | solution.py:38
  210.8 11.5 %collective-permute-start.30 = (bf16[48,1920]{1,0:T(8,128)(2,1)S(1)}, bf16[48,1920]{1,0:T(8,128)(2,1)S(1)}, u32[]{:S(2)}, u32[]{:S(2)}) collective-permute-start(bf16[48,1920]{1,0:T(8,128)(2,1)S(1)} %get-tuple-element.84), channel_id=1, source_target_pairs={{0,3},{1,2},{2,1},{3,0},{4,7},{5,6},{6,5},{7,4},{8,11},{9,10},{10,... | collective-permute-start | bytes 552968 | tf_op jit(solution)/shard_map/ppermute | solution.py:38
  239.5 17.3 %collective-permute-start.40 = (bf16[96,576]{1,0:T(8,128)(2,1)S(1)}, bf16[96,576]{1,0:T(8,128)(2,1)S(1)}, u32[]{:S(2)}, u32[]{:S(2)}) collective-permute-start(bf16[96,576]{1,0:T(8,128)(2,1)S(1)} %fusion.44.refs_0_), channel_id=1, source_target_pairs={{0,2},{1,3},{2,0},{3,1},{4,6},{5,7},{6,4},{7,5},{8,10},{9,11},{10,... | collective-permute-start | bytes 331784 | tf_op jit(solution)/shard_map/ppermute | solution.py:38
  239.5 17.3 %collective-permute-start.35 = (f32[72,128]{1,0:T(8,128)S(1)}, f32[72,128]{1,0:T(8,128)S(1)}, u32[]{:S(2)}, u32[]{:S(2)}) collective-permute-start(f32[72,128]{1,0:T(8,128)S(1)} %add.391), channel_id=1, source_target_pairs={{0,4},{4,0},{1,5},{5,1},{2,6},{6,2},{3,7},{7,3},{8,12},{12,8},{9,1... | collective-permute-start | bytes 110600 | tf_op jit(solution)/shard_map/ppermute | solution.py:38
  241.5 17.0 %collective-permute-start.39 = (bf16[96,576]{1,0:T(8,128)(2,1)S(1)}, bf16[96,576]{1,0:T(8,128)(2,1)S(1)}, u32[]{:S(2)}, u32[]{:S(2)}) collective-permute-start(bf16[96,576]{1,0:T(8,128)(2,1)S(1)} %fusion.44.refs_0_), channel_id=1, source_target_pairs={{0,1},{1,0},{2,3},{3,2},{4,5},{5,4},{6,7},{7,6},{8,9},{9,8},{10,11... | collective-permute-start | bytes 331784 | tf_op jit(solution)/shard_map/ppermute | solution.py:38
  243.4 16.3 %collective-permute-start.48 = (bf16[48,1920]{1,0:T(8,128)(2,1)S(1)}, bf16[48,1920]{1,0:T(8,128)(2,1)S(1)}, u32[]{:S(2)}, u32[]{:S(2)}) collective-permute-start(bf16[48,1920]{1,0:T(8,128)(2,1)S(1)} %fusion.29.refs_0_), channel_id=1, source_target_pairs={{0,3},{1,2},{2,1},{3,0},{4,7},{5,6},{6,5},{7,4},{8,11},{9,10},{10,... | collective-permute-start | bytes 552968 | tf_op jit(solution)/shard_map/ppermute | solution.py:38
  245.9 18.4 %collective-permute-start.47 = (bf16[48,1920]{1,0:T(8,128)(2,1)S(1)}, bf16[48,1920]{1,0:T(8,128)(2,1)S(1)}, u32[]{:S(2)}, u32[]{:S(2)}) collective-permute-start(bf16[48,1920]{1,0:T(8,128)(2,1)S(1)} %fusion.29.refs_0_), channel_id=1, source_target_pairs={{0,2},{1,3},{2,0},{3,1},{4,6},{5,7},{6,4},{7,5},{8,10},{9,11},{10,... | collective-permute-start | bytes 552968 | tf_op jit(solution)/shard_map/ppermute | solution.py:38
  258.5 24.9 %collective-permute-start.49 = (bf16[48,1920]{1,0:T(8,128)(2,1)S(1)}, bf16[48,1920]{1,0:T(8,128)(2,1)S(1)}, u32[]{:S(2)}, u32[]{:S(2)}) collective-permute-start(bf16[48,1920]{1,0:T(8,128)(2,1)S(1)} %fusion.29.refs_0_), channel_id=1, source_target_pairs={{0,4},{4,0},{1,5},{5,1},{2,6},{6,2},{3,7},{7,3},{8,12},{12,8},{9,1... | collective-permute-start | bytes 552968 | tf_op jit(solution)/shard_map/ppermute | solution.py:38
  264.3 19.1 %collective-permute-start.52 = (bf16[48,1920]{1,0:T(8,128)(2,1)S(1)}, bf16[48,1920]{1,0:T(8,128)(2,1)S(1)}, u32[]{:S(2)}, u32[]{:S(2)}) collective-permute-start(bf16[48,1920]{1,0:T(8,128)(2,1)S(1)} %collective-permute-done.48.refs_3_), channel_id=1, source_target_pairs={{0,4},{4,0},{1,5},{5,1},{2,6},{6,2},{3,7},{7,3},{8,12},{12,8},{9,1... | collective-permute-start | bytes 552968 | tf_op jit(solution)/shard_map/ppermute | solution.py:38
  265.5 17.9 %collective-permute-start.51 = (bf16[48,1920]{1,0:T(8,128)(2,1)S(1)}, bf16[48,1920]{1,0:T(8,128)(2,1)S(1)}, u32[]{:S(2)}, u32[]{:S(2)}) collective-permute-start(bf16[48,1920]{1,0:T(8,128)(2,1)S(1)} %collective-permute-done.47.refs_2_), channel_id=1, source_target_pairs={{0,4},{4,0},{1,5},{5,1},{2,6},{6,2},{3,7},{7,3},{8,12},{12,8},{9,1... | collective-permute-start | bytes 552968 | tf_op jit(solution)/shard_map/ppermute | solution.py:38
  266.3 17.1 %collective-permute-start.50 = (bf16[48,1920]{1,0:T(8,128)(2,1)S(1)}, bf16[48,1920]{1,0:T(8,128)(2,1)S(1)}, u32[]{:S(2)}, u32[]{:S(2)}) collective-permute-start(bf16[48,1920]{1,0:T(8,128)(2,1)S(1)} %collective-permute-done.46.refs_1_), channel_id=1, source_target_pairs={{0,4},{4,0},{1,5},{5,1},{2,6},{6,2},{3,7},{7,3},{8,12},{12,8},{9,1... | collective-permute-start | bytes 552968 | tf_op jit(solution)/shard_map/ppermute | solution.py:38
  (101 other events, 774.7 us)
Sparse Core Ops, SparseCore 0:
  15.9 33.4 all-gather.2
  51.6 25.1 all-gather.4
